TPU v7x, 256 devices: a whole 4x4x8 slice. The times are simulated.
256 devices in a mesh: dp: 16 (over z_lo, y), expert: 16 (over x, z_hi, core).
Axes of the slice: x: 4, y: 4, z: 8 (z_hi: 2, z_lo: 4; z = z_hi * 4 + z_lo), core: 2. Of those that a mesh axis runs over, the one named last changes fastest.
Arguments:
- tokens: bfloat16 [512, 256, 1280], P(('dp', 'expert')), may hold values from -10 to 10, as said below
- slot_keys: bfloat16 [1280, 32], replicated, may hold values from -2 to 2
- w_in: bfloat16 [32, 1280, 5120], P('expert', None, 'dp'), may hold values from -0.15625 to 0.15625
- w_out: bfloat16 [32, 5120, 1280], P('expert', 'dp'), may hold values from -0.078125 to 0.078125
- grad_out: bfloat16 [512, 256, 1280], P(('dp', 'expert')), may hold values from -6 to 6
Outputs:
- grad_tokens: bfloat16 [512, 256, 1280], P(('dp', 'expert'))
- grad_keys: float32 [1280, 32], replicated
- grad_w_in: bfloat16 [32, 1280, 5120], P('expert', None, 'dp')
- grad_w_out: bfloat16 [32, 5120, 1280], P('expert', 'dp')
Inputs may be any that keep to these rules, and one draw needn't show every extreme that they name: `tokens`: patch features of order one.
All inputs are finite; a program needn't handle non-finite values.
Results may differ from a plain program's by a relative error of at most 0.029.
Values may be sent and summed in bfloat16 or wider, within the bound.
A program may use at most 128 MiB of HBM per device.

v0:
```python
import jax
import jax.numpy as jnp
from jax import lax
from jax.sharding import PartitionSpec as P

INV_ROOT2 = 0.7071067811865476
INV_ROOT_TWO_PI = 0.3989422804014327


def gelu_value(pre_act):
    return 0.5 * pre_act * (1.0 + jax.scipy.special.erf(pre_act * INV_ROOT2))


def gelu_slope(pre_act):
    return (
        0.5 * (1.0 + jax.scipy.special.erf(pre_act * INV_ROOT2))
        + pre_act * jnp.exp(-0.5 * pre_act * pre_act) * INV_ROOT_TWO_PI
    )


def local(tokens, slot_keys, w_in, w_out, grad_out):
    logits = jnp.einsum("bpd,ds->bps", tokens, slot_keys, preferred_element_type=jnp.float32)
    dispatch = jax.nn.softmax(logits, axis=1)
    combine = jax.nn.softmax(logits, axis=2)
    dispatch_low = dispatch.astype(jnp.bfloat16)
    combine_low = combine.astype(jnp.bfloat16)
    slot_in = jnp.einsum(
        "bps,bpd->bsd", dispatch_low, tokens, preferred_element_type=jnp.float32
    ).astype(jnp.bfloat16)
    slot_grad = jnp.einsum(
        "bps,bpd->bsd", combine_low, grad_out, preferred_element_type=jnp.float32
    ).astype(jnp.bfloat16)
    sent_in, sent_grad = (
        lax.all_to_all(slot_in, "expert", split_axis=1, concat_axis=0, tiled=True),
        lax.all_to_all(slot_grad, "expert", split_axis=1, concat_axis=0, tiled=True),
    )
    rows_in, rows_grad = (
        lax.all_gather(sent_in, "dp", axis=0, tiled=True),
        lax.all_gather(sent_grad, "dp", axis=0, tiled=True),
    )
    pre_act = jnp.einsum("rkd,kdf->rkf", rows_in, w_in, preferred_element_type=jnp.float32)
    hidden_act = gelu_value(pre_act).astype(jnp.bfloat16)
    act_grad = jnp.einsum("rkd,kfd->rkf", rows_grad, w_out, preferred_element_type=jnp.float32)
    pre_grad = (act_grad * gelu_slope(pre_act)).astype(jnp.bfloat16)
    grad_w_out = jnp.einsum(
        "rkf,rkd->kfd", hidden_act, rows_grad, preferred_element_type=jnp.float32
    ).astype(jnp.bfloat16)
    grad_w_in = jnp.einsum(
        "rkd,rkf->kdf", rows_in, pre_grad, preferred_element_type=jnp.float32
    ).astype(jnp.bfloat16)
    summed_out = lax.psum_scatter(
        jnp.einsum("rkf,kfd->rkd", hidden_act, w_out, preferred_element_type=jnp.float32).astype(
            jnp.bfloat16
        ),
        "dp",
        scatter_dimension=0,
        tiled=True,
    )
    slot_out = lax.all_to_all(summed_out, "expert", split_axis=0, concat_axis=1, tiled=True)
    summed_dx = lax.psum_scatter(
        jnp.einsum("rkf,kdf->rkd", pre_grad, w_in, preferred_element_type=jnp.float32).astype(
            jnp.bfloat16
        ),
        "dp",
        scatter_dimension=0,
        tiled=True,
    )
    slot_dx = lax.all_to_all(summed_dx, "expert", split_axis=0, concat_axis=1, tiled=True)
    comb_grad = jnp.einsum("bpd,bsd->bps", grad_out, slot_out, preferred_element_type=jnp.float32)
    comb_logit = combine * (comb_grad - jnp.sum(combine * comb_grad, axis=2, keepdims=True))
    disp_grad = jnp.einsum("bpd,bsd->bps", tokens, slot_dx, preferred_element_type=jnp.float32)
    disp_logit = dispatch * (disp_grad - jnp.sum(dispatch * disp_grad, axis=1, keepdims=True))
    logit_grad = (comb_logit + disp_logit).astype(jnp.bfloat16)
    grad_tokens = (
        jnp.einsum("bps,bsd->bpd", dispatch_low, slot_dx, preferred_element_type=jnp.float32)
        + jnp.einsum("bps,ds->bpd", logit_grad, slot_keys, preferred_element_type=jnp.float32)
    ).astype(jnp.bfloat16)
    key_terms = jnp.einsum("bpd,bps->ds", tokens, logit_grad, preferred_element_type=jnp.float32)
    grad_keys = lax.psum(key_terms, ("dp", "expert"))
    return (grad_tokens, grad_keys, grad_w_in, grad_w_out)


def solution(mesh):
    return jax.shard_map(
        local,
        mesh=mesh,
        in_specs=(
            P(("dp", "expert"), None, None),
            P(),
            P("expert", None, "dp"),
            P("expert", "dp", None),
            P(("dp", "expert"), None, None),
        ),
        out_specs=(
            P(("dp", "expert"), None, None),
            P(),
            P("expert", None, "dp"),
            P("expert", "dp", None),
        ),
        check_vma=False,
    )
```

profile of v0, /device:TPU:1, one launch (start us, length us, event | category | flops | bytes accessed | tf_op | source)
XLA Modules:
  0.0 656.0 jit_solution(14120960178781851419)
XLA Ops:
  7.2 1.9 fusion.29
  9.2 0.7 fusion.38
  10.5 22.7 %all_to_all.72 = bf16[2,32,1280]{2,0,1:T(2,128)(2,1)S(1)} all-to-all(bf16[2,32,1280]{2,0,1:T(2,128)(2,1)S(1)} %copy.15), channel_id=1, replica_groups=mesh['dp'=16,'expert'=16] {'expert'}, dimensions={1} | all-to-all | bytes 327680 | tf_op jit(solution)/shard_map/all_to_all | solution.py:34
  33.2 0.7 all_to_all.59
  34.1 0.6 fusion.37
  34.7 1.6 convolution_convert_fusion.5
  36.5 13.6 %all_to_all.73 = bf16[2,32,1280]{2,0,1:T(2,128)(2,1)S(1)} all-to-all(bf16[2,32,1280]{2,0,1:T(2,128)(2,1)S(1)} %copy.13), channel_id=1, replica_groups=mesh['dp'=16,'expert'=16] {'expert'}, dimensions={1} | all-to-all | bytes 327680 | tf_op jit(solution)/shard_map/all_to_all | solution.py:35
  50.2 0.7 all_to_all.55
  51.0 56.5 %all-gather.5.cloned.1.call-done = bf16[512,2,1280]{2,0,1:T(8,128)(2,1)} async-done(((bf16[32,2,1280]{2,0,1:T(8,128)(2,1)}), bf16[512,2,1280]{2,0,1:T(8,128)(2,1)}) %all-gather.5.cloned.1.call-update) | async-done | bytes 2621456 | tf_op jit(solution)/shard_map/all_gather | solution.py:38
  107.5 3.3 convolution_bitcast_fusion.1
  110.8 1.0 copy-done.2
  111.8 3.1 fusion.5
  115.1 78.5 %all-gather.3.cloned.1.call-done = bf16[512,2,1280]{2,0,1:T(8,128)(2,1)} async-done(((bf16[32,2,1280]{2,0,1:T(8,128)(2,1)}), bf16[512,2,1280]{2,0,1:T(8,128)(2,1)}) %all-gather.3.cloned.1.call-update) | async-done | bytes 2621456 | tf_op jit(solution)/shard_map/all_gather | solution.py:39
  193.6 3.5 fusion.8
  197.0 0.9 copy-done.3
  197.9 3.1 fusion.4
  201.0 82.5 %reduce-scatter.5.cloned.1.call-done = bf16[32,2,1280]{2,0,1:T(8,128)(2,1)} async-done(((bf16[512,2,1280]{2,0,1:T(8,128)(2,1)}), bf16[32,2,1280]{2,0,1:T(8,128)(2,1)}) %reduce-scatter.5.cloned.1.call-update) | async-done | bytes 163856 | tf_op jit(solution)/shard_map/reduce_scatter | solution.py:51
  283.5 1.8 copy.19
  285.2 17.2 %all-to-all-start.3 = ((bf16[32,2,1280]{2,1,0:T(2,128)(2,1)}), bf16[32,2,1280]{2,1,0:T(2,128)(2,1)S(1)}, u32[]{:S(2)}, u32[]{:S(2)}) async-start(bf16[32,2,1280]{2,1,0:T(2,128)(2,1)} %copy.19), calls=%async_computation.5 | async-start | bytes 327680 | tf_op jit(solution)/shard_map/all_to_all | solution.py:59
  302.4 4.4 convolution_convert_fusion.3
  306.9 64.2 %reduce-scatter.3.cloned.1.call-done = bf16[32,2,1280]{2,0,1:T(8,128)(2,1)} async-done(((bf16[512,2,1280]{2,0,1:T(8,128)(2,1)}), bf16[32,2,1280]{2,0,1:T(8,128)(2,1)}) %reduce-scatter.3.cloned.1.call-update) | async-done | bytes 163856 | tf_op jit(solution)/shard_map/reduce_scatter | solution.py:60
  371.1 1.8 copy.17
  372.9 18.9 %all-to-all-start.2 = ((bf16[32,2,1280]{2,1,0:T(2,128)(2,1)}), bf16[32,2,1280]{2,1,0:T(2,128)(2,1)S(1)}, u32[]{:S(2)}, u32[]{:S(2)}) async-start(bf16[32,2,1280]{2,1,0:T(2,128)(2,1)} %copy.17), calls=%async_computation.3 | async-start | bytes 327680 | tf_op jit(solution)/shard_map/all_to_all | solution.py:68
  391.8 4.1 convolution_convert_fusion.2
  396.1 2.4 convolution_bitcast_fusion.4
  398.6 3.5 all-to-all-done.2
  402.8 1.1 fusion.21
  403.9 2.0 convolution_bitcast_fusion
  405.8 3.0 fusion.23
  408.9 3.4 fusion.6
  412.3 235.6 %all-reduce.2.cloned.1.call-done = f32[1280,32]{0,1:T(8,128)} async-done(((f32[1280,32]{0,1:T(8,128)}), f32[1280,32]{0,1:T(8,128)}) %all-reduce.2.cloned.1.call-update) | async-done | bytes 163856 | tf_op jit(solution)/shard_map/psum | solution.py:79
  647.9 1.6 copy.30
  (31 shorter events, 2.1 us)
Async XLA Ops:
  7.2 104.7 %copy-start = (bf16[2,320,1280]{2,1,0:T(8,128)(2,1)S(1)}, bf16[2,320,1280]{2,1,0:T(8,128)(2,1)}, u32[]{:S(2)}) copy-start(bf16[2,320,1280]{2,1,0:T(8,128)(2,1)} %param.8) | copy-start | bytes 4915204
  7.2 2.7 copy-start.1
  7.2 100.3 %all-gather.5.cloned.1.call-start = ((), (), s32[]{:S(2)}) async-start(), calls=%async_computation.7 | async-start | bytes 2785280 | tf_op jit(solution)/shard_map/all_gather | solution.py:38
  34.0 159.5 %all-gather.3.cloned.1.call-start = ((), (), s32[]{:S(2)}) async-start(), calls=%async_computation.6 | async-start | bytes 2785280 | tf_op jit(solution)/shard_map/all_gather | solution.py:39
  51.0 232.5 %reduce-scatter.5.cloned.1.call-start = ((), (), s32[]{:S(2)}) async-start(), calls=%async_computation.9 | async-start | bytes 2785280 | tf_op jit(solution)/shard_map/reduce_scatter | solution.py:51
  110.8 1.1 copy-start.2
  115.0 256.1 %reduce-scatter.3.cloned.1.call-start = ((), (), s32[]{:S(2)}) async-start(), calls=%async_computation.8 | async-start | bytes 2785280 | tf_op jit(solution)/shard_map/reduce_scatter | solution.py:60
  193.6 4.3 copy-start.5
  197.0 0.9 copy-start.3
  285.2 87.6 %all-to-all-start.3 = ((bf16[32,2,1280]{2,1,0:T(2,128)(2,1)}), bf16[32,2,1280]{2,1,0:T(2,128)(2,1)S(1)}, u32[]{:S(2)}, u32[]{:S(2)}) async-start(bf16[32,2,1280]{2,1,0:T(2,128)(2,1)} %copy.19), calls=%async_computation.5 | async-start | bytes 327680 | tf_op jit(solution)/shard_map/all_to_all | solution.py:59
  372.9 29.2 %all-to-all-start.2 = ((bf16[32,2,1280]{2,1,0:T(2,128)(2,1)}), bf16[32,2,1280]{2,1,0:T(2,128)(2,1)S(1)}, u32[]{:S(2)}, u32[]{:S(2)}) async-start(bf16[32,2,1280]{2,1,0:T(2,128)(2,1)} %copy.17), calls=%async_computation.3 | async-start | bytes 327680 | tf_op jit(solution)/shard_map/all_to_all | solution.py:68
  391.8 256.1 %all-reduce.2.cloned.1.call-start = ((), (), s32[]{:S(2)}) async-start(), calls=%async_computation.10 | async-start | bytes 327680 | tf_op jit(solution)/shard_map/psum | solution.py:79
  402.8 3.1 copy-start.4
Sparse Core Ops, SparseCore 0:
  34.1 73.3 all-gather.4
  109.9 83.6 all-gather.2
  196.1 87.3 reduce-scatter.4
  285.9 85.1 reduce-scatter.2
  409.0 238.8 all-reduce.1
where the time goes:
time: 657 us; the launch traced here: 656 us
  waiting for transfers between devices  521 us (79%)
  matrix products  36.7 us (6%)
  starting transfers between devices  36.3 us (6%)
  blocking collectives  36.2 us (6%)
  between operations  13.9 us (2%)
  local copies, waits for them, and re-layouts  9.43 us (1%)
    psum x1, waiting for transfers between devices, local(): grad_keys = lax.psum(key_terms, ('dp', 'expert'))  236 us
    reduce_scatter x1, waiting for transfers between devices, local(): lax.psum_scatter(jnp.einsum('rkf,kfd->rkd', hidden_act, w_out, preferred_...  82.5 us
    all_gather x1, waiting for transfers between devices, local(): lax.all_gather(sent_grad, 'dp', axis=0, tiled=True)  78.5 us
    reduce_scatter x1, waiting for transfers between devices, local(): lax.psum_scatter(jnp.einsum('rkf,kdf->rkd', pre_grad, w_in, preferred_ele...  64.2 us
    all_gather x1, waiting for transfers between devices, local(): lax.all_gather(sent_in, 'dp', axis=0, tiled=True)  56.5 us
    all_to_all x1, blocking collectives, local(): lax.all_to_all(slot_in, 'expert', split_axis=1, concat_axis=0, tiled=True)  22.7 us
    all_to_all x1, starting transfers between devices, local(): lax.all_to_all(summed_dx, 'expert', split_axis=0, concat_axis=1, tiled=True)  18.9 us
    all_to_all x1, starting transfers between devices, local(): lax.all_to_all(summed_out, 'expert', split_axis=0, concat_axis=1, tiled=T...  17.2 us
  transfers between devices with their start and end apart: 7, of which 6 were waited for; matrix products, arithmetic and copies ran while one was open for 5% of the time, Pallas kernels for 0%

commit v1 on v0

--- a/solution.py
+++ b/solution.py
@@ -1,7 +1,12 @@
 import jax
 import jax.numpy as jnp
 from jax import lax
+from jax.experimental import pallas as pl
+from jax.experimental.pallas import tpu as pltpu
 from jax.sharding import PartitionSpec as P
+
+MESH = pl.DeviceIdType.MESH
+GROUP = 16
 
 INV_ROOT2 = 0.7071067811865476
 INV_ROOT_TWO_PI = 0.3989422804014327
@@ -16,6 +21,102 @@
         0.5 * (1.0 + jax.scipy.special.erf(pre_act * INV_ROOT2))
         + pre_act * jnp.exp(-0.5 * pre_act * pre_act) * INV_ROOT_TWO_PI
     )
+
+
+def sum_kernel(x_ref, out_ref, src, landed_a, landed_b, part, total, send, recv):
+    row, col = lax.axis_index("dp"), lax.axis_index("expert")
+
+    def at(axis, offset):
+        if axis == 0:
+            return (lax.rem(row + offset, GROUP), col)
+        return (row, lax.rem(col + offset, GROUP))
+
+    barrier = pltpu.get_barrier_semaphore()
+
+    @pl.loop(1, GROUP)
+    def _(o):
+        for axis in range(2):
+            pl.semaphore_signal(barrier, inc=1, device_id=at(axis, o), device_id_type=MESH)
+
+    tiles = x_ref.shape[0]
+    src[pl.ds(0, tiles)] = x_ref[...]
+    src[pl.ds(tiles, src.shape[0] - tiles)] = jnp.zeros(
+        (src.shape[0] - tiles,) + src.shape[1:], src.dtype
+    )
+    pl.semaphore_wait(barrier, 2 * (GROUP - 1))
+
+    def copy(round_, o):
+        if round_ == 0:
+            there = at(0, o)
+            a, b = src.at[pl.ds(3 * there[0], 3)], landed_a.at[o]
+        elif round_ == 1:
+            there = at(1, o)
+            a, b = part, landed_b.at[o]
+        else:
+            there = at(0, o)
+            a, b = total, out_ref.at[row]
+        return pltpu.make_async_remote_copy(
+            src_ref=a,
+            dst_ref=b,
+            send_sem=send.at[round_, o],
+            recv_sem=recv.at[round_, o],
+            device_id=there,
+            device_id_type=MESH,
+        )
+
+    def start(round_):
+        @pl.loop(1, GROUP)
+        def _(o):
+            copy(round_, o).start()
+
+    def finish(round_):
+        @pl.loop(1, GROUP)
+        def _(o):
+            copy(round_, o).wait_recv()
+
+    start(0)
+    finish(0)
+    acc = src[pl.ds(3 * row, 3)]
+    for o in range(1, GROUP):
+        acc = acc + landed_a[o]
+    part[...] = acc
+    start(1)
+    finish(1)
+    acc = jnp.zeros(part.shape, part.dtype)
+    landed_b[0] = part[...]
+    for c in range(GROUP):
+        acc = acc + landed_b[lax.rem(col - c + GROUP, GROUP)]
+    total[...] = acc
+    start(2)
+    out_ref[row] = acc
+    finish(2)
+
+    @pl.loop(1, GROUP)
+    def _(o):
+        for r in range(3):
+            copy(r, o).wait_send()
+
+
+def sum_over_devices(x):
+    chunk = (3, 8, 128)
+    out = pl.pallas_call(
+        sum_kernel,
+        out_shape=jax.ShapeDtypeStruct((GROUP,) + chunk, jnp.float32),
+        in_specs=[pl.BlockSpec(memory_space=pltpu.VMEM)],
+        out_specs=pl.BlockSpec(memory_space=pltpu.VMEM),
+        scratch_shapes=[
+            pltpu.VMEM((3 * GROUP, 8, 128), jnp.float32),
+            pltpu.VMEM((GROUP,) + chunk, jnp.float32),
+            pltpu.VMEM((GROUP,) + chunk, jnp.float32),
+            pltpu.VMEM(chunk, jnp.float32),
+            pltpu.VMEM(chunk, jnp.float32),
+            pltpu.SemaphoreType.DMA((3, GROUP)),
+            pltpu.SemaphoreType.DMA((3, GROUP)),
+        ],
+        compiler_params=pltpu.CompilerParams(collective_id=1, has_side_effects=True),
+        name="sum_keys",
+    )(x)
+    return out.reshape(3 * GROUP, 8, 128)[: x.shape[0]]
 
 
 def local(tokens, slot_keys, w_in, w_out, grad_out):
@@ -75,8 +176,12 @@
         jnp.einsum("bps,bsd->bpd", dispatch_low, slot_dx, preferred_element_type=jnp.float32)
         + jnp.einsum("bps,ds->bpd", logit_grad, slot_keys, preferred_element_type=jnp.float32)
     ).astype(jnp.bfloat16)
-    key_terms = jnp.einsum("bpd,bps->ds", tokens, logit_grad, preferred_element_type=jnp.float32)
-    grad_keys = lax.psum(key_terms, ("dp", "expert"))
+    key_terms = jnp.einsum("bpd,bps->sd", tokens, logit_grad, preferred_element_type=jnp.float32)
+    slots, width = key_terms.shape
+    tiles = key_terms.reshape(slots // 8, 8, width // 128, 128).transpose(0, 2, 1, 3)
+    summed = sum_over_devices(tiles.reshape(-1, 8, 128))
+    summed = summed.reshape(slots // 8, width // 128, 8, 128).transpose(0, 2, 1, 3)
+    grad_keys = summed.reshape(slots, width).T
     return (grad_tokens, grad_keys, grad_w_in, grad_w_out)
 
 

time: 657 us -> 447 us (0.68)
  waiting for transfers between devices: 521 us -> 285 us
  Pallas kernels: 0 us -> 25.4 us
    psum x1 -> x0, waiting for transfers between devices: 236 us -> none  [local(): grad_keys = lax.psum(key_terms, ('dp', 'expert'))]
    pallas_call x0 -> x1, Pallas kernels: none -> 25.4 us  [sum_over_devices(): pl.pallas_call(sum_kernel, out_shape=jax.ShapeDtypeStruct((GROUP,) + chun...]
  transfers between devices with their start and end apart: 7 -> 6, of which waited for: 6 -> 5; matrix products, arithmetic and copies ran while one was open for 5% -> 7% of each run, Pallas kernels for 0% -> 0%
where the time goes in v1:
time: 447 us; the launch traced here: 446 us
  waiting for transfers between devices  285 us (64%)
  matrix products  36.7 us (8%)
  starting transfers between devices  36.3 us (8%)
  blocking collectives  36.2 us (8%)
  Pallas kernels  25.4 us (6%)
  between operations  13.9 us (3%)
  local copies, waits for them, and re-layouts  9.43 us (2%)
    reduce_scatter x1, waiting for transfers between devices, local(): lax.psum_scatter(jnp.einsum('rkf,kfd->rkd', hidden_act, w_out, preferred_...  82.5 us
    all_gather x1, waiting for transfers between devices, local(): lax.all_gather(sent_grad, 'dp', axis=0, tiled=True)  78.5 us
    reduce_scatter x1, waiting for transfers between devices, local(): lax.psum_scatter(jnp.einsum('rkf,kdf->rkd', pre_grad, w_in, preferred_ele...  64.2 us
    all_gather x1, waiting for transfers between devices, local(): lax.all_gather(sent_in, 'dp', axis=0, tiled=True)  56.5 us
    pallas_call x1, Pallas kernels, sum_over_devices(): pl.pallas_call(sum_kernel, out_shape=jax.ShapeDtypeStruct((GROUP,) + chun...  25.4 us
    all_to_all x1, blocking collectives, local(): lax.all_to_all(slot_in, 'expert', split_axis=1, concat_axis=0, tiled=True)  22.7 us
    all_to_all x1, starting transfers between devices, local(): lax.all_to_all(summed_dx, 'expert', split_axis=0, concat_axis=1, tiled=True)  18.9 us
    all_to_all x1, starting transfers between devices, local(): lax.all_to_all(summed_out, 'expert', split_axis=0, concat_axis=1, tiled=T...  17.2 us
  transfers between devices with their start and end apart: 6, of which 5 were waited for; matrix products, arithmetic and copies ran while one was open for 7% of the time, Pallas kernels for 0%

profile of v1, /device:TPU:1, one launch (start us, length us, event | category | flops | bytes accessed | tf_op | source)
XLA Modules:
  0.0 445.8 jit_solution(1100508430507972935)
XLA Ops:
  7.2 1.9 fusion.30
  9.2 0.7 fusion.39
  10.5 22.7 %all_to_all.72 = bf16[2,32,1280]{2,0,1:T(2,128)(2,1)S(1)} all-to-all(bf16[2,32,1280]{2,0,1:T(2,128)(2,1)S(1)} %copy.15), channel_id=1, replica_groups=mesh['dp'=16,'expert'=16] {'expert'}, dimensions={1} | all-to-all | bytes 327680 | tf_op jit(solution)/shard_map/all_to_all | solution.py:135
  33.2 0.7 all_to_all.59
  34.1 0.6 fusion.38
  34.7 1.6 convolution_convert_fusion.5
  36.5 13.6 %all_to_all.73 = bf16[2,32,1280]{2,0,1:T(2,128)(2,1)S(1)} all-to-all(bf16[2,32,1280]{2,0,1:T(2,128)(2,1)S(1)} %copy.13), channel_id=1, replica_groups=mesh['dp'=16,'expert'=16] {'expert'}, dimensions={1} | all-to-all | bytes 327680 | tf_op jit(solution)/shard_map/all_to_all | solution.py:136
  50.2 0.7 all_to_all.55
  51.0 56.5 %all-gather.5.cloned.1.call-done = bf16[512,2,1280]{2,0,1:T(8,128)(2,1)} async-done(((bf16[32,2,1280]{2,0,1:T(8,128)(2,1)}), bf16[512,2,1280]{2,0,1:T(8,128)(2,1)}) %all-gather.5.cloned.1.call-update) | async-done | bytes 2621456 | tf_op jit(solution)/shard_map/all_gather | solution.py:139
  107.5 3.3 convolution_bitcast_fusion
  110.8 1.0 copy-done.2
  111.8 3.1 fusion.5
  115.1 78.5 %all-gather.3.cloned.1.call-done = bf16[512,2,1280]{2,0,1:T(8,128)(2,1)} async-done(((bf16[32,2,1280]{2,0,1:T(8,128)(2,1)}), bf16[512,2,1280]{2,0,1:T(8,128)(2,1)}) %all-gather.3.cloned.1.call-update) | async-done | bytes 2621456 | tf_op jit(solution)/shard_map/all_gather | solution.py:140
  193.6 3.5 fusion.8
  197.0 0.9 copy-done.3
  197.9 3.1 fusion.4
  201.0 82.5 %reduce-scatter.5.cloned.1.call-done = bf16[32,2,1280]{2,0,1:T(8,128)(2,1)} async-done(((bf16[512,2,1280]{2,0,1:T(8,128)(2,1)}), bf16[32,2,1280]{2,0,1:T(8,128)(2,1)}) %reduce-scatter.5.cloned.1.call-update) | async-done | bytes 163856 | tf_op jit(solution)/shard_map/reduce_scatter | solution.py:152
  283.5 1.8 copy.19
  285.2 17.2 %all-to-all-start.3 = ((bf16[32,2,1280]{2,1,0:T(2,128)(2,1)}), bf16[32,2,1280]{2,1,0:T(2,128)(2,1)S(1)}, u32[]{:S(2)}, u32[]{:S(2)}) async-start(bf16[32,2,1280]{2,1,0:T(2,128)(2,1)} %copy.19), calls=%async_computation.5 | async-start | bytes 327680 | tf_op jit(solution)/shard_map/all_to_all | solution.py:160
  302.4 4.4 convolution_convert_fusion.3
  306.9 64.2 %reduce-scatter.3.cloned.1.call-done = bf16[32,2,1280]{2,0,1:T(8,128)(2,1)} async-done(((bf16[512,2,1280]{2,0,1:T(8,128)(2,1)}), bf16[32,2,1280]{2,0,1:T(8,128)(2,1)}) %reduce-scatter.3.cloned.1.call-update) | async-done | bytes 163856 | tf_op jit(solution)/shard_map/reduce_scatter | solution.py:161
  371.1 1.8 copy.17
  372.9 18.9 %all-to-all-start.2 = ((bf16[32,2,1280]{2,1,0:T(2,128)(2,1)}), bf16[32,2,1280]{2,1,0:T(2,128)(2,1)S(1)}, u32[]{:S(2)}, u32[]{:S(2)}) async-start(bf16[32,2,1280]{2,1,0:T(2,128)(2,1)} %copy.17), calls=%async_computation.3 | async-start | bytes 327680 | tf_op jit(solution)/shard_map/all_to_all | solution.py:169
  391.8 4.1 convolution_convert_fusion.2
  396.1 2.4 convolution_bitcast_fusion.3
  398.5 3.6 all-to-all-done.2
  402.8 1.1 fusion.21
  403.9 2.0 fusion.23
  405.8 3.0 fusion.24
  408.8 25.4 %sum_keys.1 = f32[16,3,8,128]{3,2,1,0:T(8,128)} custom-call(f32[40,8,128]{2,1,0:T(8,128)} %bitcast.81), custom_call_target="tpu_custom_call" | custom-call | tf_op jit(solution)/shard_map/sum_keys/pallas_call | solution.py:102
  434.3 1.6 slice.4
  435.9 3.4 fusion.6
  (29 shorter events, 2.0 us)
Async XLA Ops:
  7.2 104.7 %copy-start = (bf16[2,320,1280]{2,1,0:T(8,128)(2,1)S(1)}, bf16[2,320,1280]{2,1,0:T(8,128)(2,1)}, u32[]{:S(2)}) copy-start(bf16[2,320,1280]{2,1,0:T(8,128)(2,1)} %param.8) | copy-start | bytes 4915204
  7.2 2.7 copy-start.1
  7.2 100.3 %all-gather.5.cloned.1.call-start = ((), (), s32[]{:S(2)}) async-start(), calls=%async_computation.7 | async-start | bytes 2785280 | tf_op jit(solution)/shard_map/all_gather | solution.py:139
  34.0 159.5 %all-gather.3.cloned.1.call-start = ((), (), s32[]{:S(2)}) async-start(), calls=%async_computation.6 | async-start | bytes 2785280 | tf_op jit(solution)/shard_map/all_gather | solution.py:140
  51.0 232.5 %reduce-scatter.5.cloned.1.call-start = ((), (), s32[]{:S(2)}) async-start(), calls=%async_computation.9 | async-start | bytes 2785280 | tf_op jit(solution)/shard_map/reduce_scatter | solution.py:152
  110.8 1.1 copy-start.2
  115.0 256.1 %reduce-scatter.3.cloned.1.call-start = ((), (), s32[]{:S(2)}) async-start(), calls=%async_computation.8 | async-start | bytes 2785280 | tf_op jit(solution)/shard_map/reduce_scatter | solution.py:161
  193.6 4.3 copy-start.5
  197.0 0.9 copy-start.3
  285.2 87.6 %all-to-all-start.3 = ((bf16[32,2,1280]{2,1,0:T(2,128)(2,1)}), bf16[32,2,1280]{2,1,0:T(2,128)(2,1)S(1)}, u32[]{:S(2)}, u32[]{:S(2)}) async-start(bf16[32,2,1280]{2,1,0:T(2,128)(2,1)} %copy.19), calls=%async_computation.5 | async-start | bytes 327680 | tf_op jit(solution)/shard_map/all_to_all | solution.py:160
  372.9 29.2 %all-to-all-start.2 = ((bf16[32,2,1280]{2,1,0:T(2,128)(2,1)}), bf16[32,2,1280]{2,1,0:T(2,128)(2,1)S(1)}, u32[]{:S(2)}, u32[]{:S(2)}) async-start(bf16[32,2,1280]{2,1,0:T(2,128)(2,1)} %copy.17), calls=%async_computation.3 | async-start | bytes 327680 | tf_op jit(solution)/shard_map/all_to_all | solution.py:169
  402.8 3.1 copy-start.4
Sparse Core Ops, SparseCore 0:
  34.1 73.3 all-gather.4
  109.9 83.6 all-gather.2
  196.1 87.3 reduce-scatter.4
  285.9 85.1 reduce-scatter.2

commit v2 on v1

--- a/solution.py
+++ b/solution.py
@@ -7,20 +7,14 @@
 
 MESH = pl.DeviceIdType.MESH
 GROUP = 16
+Z, Y = 4, 4
+D = 1280
+HID = 320
+HALF = D // 2
+PIECE = 16
 
 INV_ROOT2 = 0.7071067811865476
 INV_ROOT_TWO_PI = 0.3989422804014327
-
-
-def gelu_value(pre_act):
-    return 0.5 * pre_act * (1.0 + jax.scipy.special.erf(pre_act * INV_ROOT2))
-
-
-def gelu_slope(pre_act):
-    return (
-        0.5 * (1.0 + jax.scipy.special.erf(pre_act * INV_ROOT2))
-        + pre_act * jnp.exp(-0.5 * pre_act * pre_act) * INV_ROOT_TWO_PI
-    )
 
 
 def sum_kernel(x_ref, out_ref, src, landed_a, landed_b, part, total, send, recv):
@@ -119,6 +113,284 @@
     return out.reshape(3 * GROUP, 8, 128)[: x.shape[0]]
 
 
+def exchange_kernel(
+    pieces_ref, w_in_ref, w_out_ref,
+    back_ref, grad_in_ref, grad_out_ref,
+    landed, rows, part, hid, pre, from_left, from_right, sum_left, sum_right, sum_z,
+    ready, send_x, recv_x, send_b, recv_b, send_z, recv_z, send_y, recv_y, send_h, recv_h,
+    send_p, recv_p, send_f, recv_f, send_s, recv_s,
+):
+    row, col = lax.axis_index("dp"), lax.axis_index("expert")
+    zz, yy = row // Y, lax.rem(row, Y)
+
+    def on_expert(o):
+        return (row, lax.rem(col + o, GROUP))
+
+    def on_z(q):
+        return (lax.rem(zz + q, Z) * Y + yy, col)
+
+    def on_y(o):
+        return (zz * Y + lax.rem(yy + o + Y, Y), col)
+
+    right, left = on_y(1), on_y(-1)
+
+    def remote(src, dst, send, recv, device):
+        return pltpu.make_async_remote_copy(
+            src_ref=src, dst_ref=dst, send_sem=send, recv_sem=recv,
+            device_id=device, device_id_type=MESH,
+        )
+
+    barrier = pltpu.get_barrier_semaphore()
+
+    @pl.loop(1, GROUP)
+    def _(o):
+        pl.semaphore_signal(barrier, inc=1, device_id=on_expert(o), device_id_type=MESH)
+
+    for q in range(1, Z):
+        pl.semaphore_signal(barrier, inc=1, device_id=on_z(q), device_id_type=MESH)
+    pl.semaphore_signal(barrier, inc=1, device_id=right, device_id_type=MESH)
+    pl.semaphore_signal(barrier, inc=1, device_id=left, device_id_type=MESH)
+    pl.semaphore_wait(barrier, GROUP - 1 + Z - 1 + 2)
+
+    def piece_out(o):
+        there = on_expert(o)
+        return remote(pieces_ref.at[there[1]], landed.at[col], send_x.at[o], recv_x.at[o], there)
+
+    @pl.loop(1, GROUP)
+    def _(o):
+        piece_out(o).start()
+
+    landed[col] = pieces_ref[col]
+
+    @pl.loop(1, GROUP)
+    def _(o):
+        piece_out(o).wait_recv()
+
+    size = GROUP * PIECE
+    r = lax.broadcasted_iota(jnp.int32, (size, size), 0)
+    c = lax.broadcasted_iota(jnp.int32, (size, size), 1)
+    home = ((r >> 1) & 15) * 16 + (r >> 5) * 2 + (r & 1)
+    turn = (c == home).astype(jnp.bfloat16)
+    block = jnp.dot(
+        turn, landed[...].reshape(size, HALF), preferred_element_type=jnp.float32
+    ).astype(jnp.bfloat16)
+    for h in range(2):
+        for t in range(2):
+            for s in range(2):
+                k = ((h * 2 + t) * 2 + s) * 32
+                rows[zz, yy, t, s, :, h * HALF : (h + 1) * HALF] = block[k : k + 32]
+
+    def place(q):
+        return lax.rem(zz - q + Z, Z)
+
+    def along_z(q):
+        mine = rows.at[zz, yy]
+        return remote(mine, mine, send_z.at[q], recv_z.at[q], on_z(q))
+
+    def along_y(q, d):
+        mine = rows.at[place(q), yy]
+        return remote(mine, mine, send_y.at[q, d], recv_y.at[q, d], left if d else right)
+
+    def onward(q, d):
+        ours = rows.at[place(q), lax.rem(yy + (1 if d else Y - 1), Y), d]
+        return remote(ours, ours, send_h.at[q, d], recv_h.at[q, d], left if d else right)
+
+    def experts(q):
+        p = place(q)
+        for s in range(2):
+            x = rows[p, :, 0, s].reshape(Y * 32, D)
+            g = rows[p, :, 1, s].reshape(Y * 32, D)
+            pre_act = jnp.dot(x, w_in_ref[s], preferred_element_type=jnp.float32)
+            act_grad = lax.dot_general(
+                g, w_out_ref[s], (((1,), (1,)), ((), ())), preferred_element_type=jnp.float32
+            )
+            cdf = 0.5 * (1.0 + lax.erf(pre_act * INV_ROOT2))
+            hidden = (pre_act * cdf).astype(jnp.bfloat16)
+            slope = cdf + pre_act * jnp.exp(-0.5 * pre_act * pre_act) * INV_ROOT_TWO_PI
+            pre_grad = (act_grad * slope).astype(jnp.bfloat16)
+            hid[s, p] = hidden
+            pre[s, p] = pre_grad
+            out = jnp.dot(hidden, w_out_ref[s], preferred_element_type=jnp.float32)
+            part[p, :, 0, s] = out.astype(jnp.bfloat16).reshape(Y, 32, D)
+            back = lax.dot_general(
+                pre_grad, w_in_ref[s], (((1,), (1,)), ((), ())), preferred_element_type=jnp.float32
+            )
+            part[p, :, 1, s] = back.astype(jnp.bfloat16).reshape(Y, 32, D)
+
+    def far(q, d):
+        ours = part.at[place(q), lax.rem(yy + 2, Y), d]
+        land = (from_right if d else from_left).at[q]
+        return remote(ours, land, send_f.at[q, d], recv_f.at[q, d], left if d else right)
+
+    def near(q, d):
+        ours = part.at[place(q), lax.rem(yy + (Y - 1 if d else 1), Y)]
+        land = (sum_right if d else sum_left).at[q]
+        return remote(ours, land, send_p.at[q, d], recv_p.at[q, d], left if d else right)
+
+    def along_z_back(q):
+        there = (place(q) * Y + yy, col)
+        return remote(part.at[place(q), yy], sum_z.at[q], send_s.at[q], recv_s.at[q], there)
+
+    def add(target, other):
+        total = target[...].astype(jnp.float32) + other[...].astype(jnp.float32)
+        target[...] = total.astype(jnp.bfloat16)
+
+    def pass_on(q):
+        for d in range(2):
+            far(q, d).wait_recv()
+            far(q, d).wait_send()
+            ours = part.at[place(q), lax.rem(yy + (Y - 1 if d else 1), Y), d]
+            add(ours, (from_right if d else from_left).at[q])
+            near(q, d).start()
+
+    def collect(q):
+        for d in range(2):
+            near(q, d).wait_recv()
+        target = part.at[place(q), yy]
+        total = (
+            target[...].astype(jnp.float32)
+            + sum_left[q].astype(jnp.float32)
+            + sum_right[q].astype(jnp.float32)
+        )
+        target[...] = total.astype(jnp.bfloat16)
+        if q > 0:
+            along_z_back(q).start()
+
+    for q in range(1, Z):
+        along_z(q).start()
+    for d in range(2):
+        along_y(0, d).start()
+
+    order = (0, 1, 2, 3)
+    for step in range(Z):
+        if step + 1 < Z:
+            along_z(step + 1).wait_recv()
+            for d in range(2):
+                along_y(step + 1, d).start()
+        for d in range(2):
+            along_y(step, d).wait_recv()
+            onward(step, d).start()
+        for d in range(2):
+            onward(step, d).wait_recv()
+        experts(step)
+        for d in range(2):
+            far(step, d).start()
+        if step >= 1:
+            pass_on(step - 1)
+        if step >= 2:
+            collect(step - 2)
+
+    def weights():
+        for s in range(2):
+            p_all = pre[s].reshape(Z * Y * 32, HID)
+            h_all = hid[s].reshape(Z * Y * 32, HID)
+            for k in range(0, D, 256):
+                x = rows[:, :, 0, s, :, k : k + 256].reshape(Z * Y * 32, 256)
+                g = rows[:, :, 1, s, :, k : k + 256].reshape(Z * Y * 32, 256)
+                grad_in_ref[s, k : k + 256, :] = lax.dot_general(
+                    x, p_all, (((0,), (0,)), ((), ())), preferred_element_type=jnp.float32
+                ).astype(jnp.bfloat16)
+                grad_out_ref[s, :, k : k + 256] = lax.dot_general(
+                    h_all, g, (((0,), (0,)), ((), ())), preferred_element_type=jnp.float32
+                ).astype(jnp.bfloat16)
+
+    weights()
+    pass_on(Z - 1)
+    collect(Z - 2)
+    collect(Z - 1)
+
+    for q in range(1, Z):
+        along_z_back(q).wait_recv()
+    mine = part.at[zz, yy]
+    total = mine[...].astype(jnp.float32)
+    for q in range(1, Z):
+        total = total + sum_z[q].astype(jnp.float32)
+    total = total.astype(jnp.bfloat16)
+    stack = jnp.concatenate(
+        [
+            total[t, s, :, h * HALF : (h + 1) * HALF]
+            for h in range(2)
+            for t in range(2)
+            for s in range(2)
+        ],
+        axis=0,
+    )
+    home = (r & 1) * 1 + (r >> 4) * 2 + ((r >> 1) & 7) * 32
+    turn = (c == home).astype(jnp.bfloat16)
+    ready[...] = (
+        jnp.dot(turn, stack, preferred_element_type=jnp.float32)
+        .astype(jnp.bfloat16)
+        .reshape(GROUP, PIECE, HALF)
+    )
+
+    def piece_back(o):
+        there = on_expert(o)
+        return remote(ready.at[there[1]], back_ref.at[col], send_b.at[o], recv_b.at[o], there)
+
+    @pl.loop(1, GROUP)
+    def _(o):
+        piece_back(o).start()
+
+    back_ref[col] = ready[col]
+
+    @pl.loop(1, GROUP)
+    def _(o):
+        piece_back(o).wait_recv()
+
+    @pl.loop(1, GROUP)
+    def _(o):
+        piece_out(o).wait_send()
+        piece_back(o).wait_send()
+
+    for q in range(Z):
+        if q > 0:
+            along_z(q).wait_send()
+            along_z_back(q).wait_send()
+        for d in range(2):
+            along_y(q, d).wait_send()
+            onward(q, d).wait_send()
+            near(q, d).wait_send()
+
+
+def expert_exchange(pieces, w_in, w_out):
+    block = (2, 2, 32, D)
+    bf16 = jnp.bfloat16
+    dma = pltpu.SemaphoreType.DMA
+    vmem = pl.BlockSpec(memory_space=pltpu.VMEM)
+    return pl.pallas_call(
+        exchange_kernel,
+        out_shape=(
+            jax.ShapeDtypeStruct(pieces.shape, bf16),
+            jax.ShapeDtypeStruct(w_in.shape, bf16),
+            jax.ShapeDtypeStruct(w_out.shape, bf16),
+        ),
+        in_specs=[vmem] * 3,
+        out_specs=(vmem,) * 3,
+        scratch_shapes=[
+            pltpu.VMEM(pieces.shape, bf16),
+            pltpu.VMEM((Z, Y) + block, bf16),
+            pltpu.VMEM((Z, Y) + block, bf16),
+            pltpu.VMEM((2, Z, Y * 32, HID), bf16),
+            pltpu.VMEM((2, Z, Y * 32, HID), bf16),
+            pltpu.VMEM((Z,) + block[1:], bf16),
+            pltpu.VMEM((Z,) + block[1:], bf16),
+            pltpu.VMEM((Z,) + block, bf16),
+            pltpu.VMEM((Z,) + block, bf16),
+            pltpu.VMEM((Z,) + block, bf16),
+            pltpu.VMEM(pieces.shape, bf16),
+            dma((GROUP,)), dma((GROUP,)), dma((GROUP,)), dma((GROUP,)),
+            dma((Z,)), dma((Z,)),
+            dma((Z, 2)), dma((Z, 2)), dma((Z, 2)), dma((Z, 2)),
+            dma((Z, 2)), dma((Z, 2)), dma((Z, 2)), dma((Z, 2)),
+            dma((Z,)), dma((Z,)),
+        ],
+        compiler_params=pltpu.CompilerParams(
+            collective_id=0, has_side_effects=True, vmem_limit_bytes=56 * 1024 * 1024
+        ),
+        name="experts",
+    )(pieces, w_in, w_out)
+
+
 def local(tokens, slot_keys, w_in, w_out, grad_out):
     logits = jnp.einsum("bpd,ds->bps", tokens, slot_keys, preferred_element_type=jnp.float32)
     dispatch = jax.nn.softmax(logits, axis=1)
@@ -131,42 +403,12 @@
     slot_grad = jnp.einsum(
         "bps,bpd->bsd", combine_low, grad_out, preferred_element_type=jnp.float32
     ).astype(jnp.bfloat16)
-    sent_in, sent_grad = (
-        lax.all_to_all(slot_in, "expert", split_axis=1, concat_axis=0, tiled=True),
-        lax.all_to_all(slot_grad, "expert", split_axis=1, concat_axis=0, tiled=True),
-    )
-    rows_in, rows_grad = (
-        lax.all_gather(sent_in, "dp", axis=0, tiled=True),
-        lax.all_gather(sent_grad, "dp", axis=0, tiled=True),
-    )
-    pre_act = jnp.einsum("rkd,kdf->rkf", rows_in, w_in, preferred_element_type=jnp.float32)
-    hidden_act = gelu_value(pre_act).astype(jnp.bfloat16)
-    act_grad = jnp.einsum("rkd,kfd->rkf", rows_grad, w_out, preferred_element_type=jnp.float32)
-    pre_grad = (act_grad * gelu_slope(pre_act)).astype(jnp.bfloat16)
-    grad_w_out = jnp.einsum(
-        "rkf,rkd->kfd", hidden_act, rows_grad, preferred_element_type=jnp.float32
-    ).astype(jnp.bfloat16)
-    grad_w_in = jnp.einsum(
-        "rkd,rkf->kdf", rows_in, pre_grad, preferred_element_type=jnp.float32
-    ).astype(jnp.bfloat16)
-    summed_out = lax.psum_scatter(
-        jnp.einsum("rkf,kfd->rkd", hidden_act, w_out, preferred_element_type=jnp.float32).astype(
-            jnp.bfloat16
-        ),
-        "dp",
-        scatter_dimension=0,
-        tiled=True,
-    )
-    slot_out = lax.all_to_all(summed_out, "expert", split_axis=0, concat_axis=1, tiled=True)
-    summed_dx = lax.psum_scatter(
-        jnp.einsum("rkf,kdf->rkd", pre_grad, w_in, preferred_element_type=jnp.float32).astype(
-            jnp.bfloat16
-        ),
-        "dp",
-        scatter_dimension=0,
-        tiled=True,
-    )
-    slot_dx = lax.all_to_all(summed_dx, "expert", split_axis=0, concat_axis=1, tiled=True)
+    images, slots, width = slot_in.shape
+    pieces = jnp.stack([slot_in, slot_grad]).reshape(2, images, GROUP, slots // GROUP, 2, HALF)
+    pieces = pieces.transpose(2, 4, 0, 3, 1, 5).reshape(GROUP, PIECE, HALF)
+    back, grad_w_in, grad_w_out = expert_exchange(pieces, w_in, w_out)
+    back = back.reshape(GROUP, 2, 2, slots // GROUP, images, HALF).transpose(2, 4, 0, 3, 1, 5)
+    slot_out, slot_dx = back.reshape(2, images, slots, width)
     comb_grad = jnp.einsum("bpd,bsd->bps", grad_out, slot_out, preferred_element_type=jnp.float32)
     comb_logit = combine * (comb_grad - jnp.sum(combine * comb_grad, axis=2, keepdims=True))
     disp_grad = jnp.einsum("bpd,bsd->bps", tokens, slot_dx, preferred_element_type=jnp.float32)
@@ -177,7 +419,6 @@
         + jnp.einsum("bps,ds->bpd", logit_grad, slot_keys, preferred_element_type=jnp.float32)
     ).astype(jnp.bfloat16)
     key_terms = jnp.einsum("bpd,bps->sd", tokens, logit_grad, preferred_element_type=jnp.float32)
-    slots, width = key_terms.shape
     tiles = key_terms.reshape(slots // 8, 8, width // 128, 128).transpose(0, 2, 1, 3)
     summed = sum_over_devices(tiles.reshape(-1, 8, 128))
     summed = summed.reshape(slots // 8, width // 128, 8, 128).transpose(0, 2, 1, 3)

time: 447 us -> 221 us (0.49)
  waiting for transfers between devices: 285 us -> 0 us
  Pallas kernels: 25.4 us -> 190 us
  starting transfers between devices: 36.3 us -> 0 us
  blocking collectives: 36.2 us -> 0 us
  matrix products: 36.7 us -> 12.3 us
  between operations: 13.9 us -> 0.75 us
    pallas_call x0 -> x1, Pallas kernels: none -> 165 us  [expert_exchange(): pl.pallas_call(exchange_kernel, out_shape=(jax.ShapeDtypeStruct(pieces.sh...]
    reduce_scatter x2 -> x0, waiting for transfers between devices: 147 us -> none  [the longest x1 82.5 us: local(): lax.psum_scatter(jnp.einsum('rkf,kfd->rkd', hidden_act, w_out, preferred_...]
    all_gather x2 -> x0, waiting for transfers between devices: 135 us -> none  [the longest x1 78.5 us: local(): lax.all_gather(sent_grad, 'dp', axis=0, tiled=True)]
    all_to_all x2 -> x0, blocking collectives: 36.2 us -> none  [the longest x1 22.7 us: local(): lax.all_to_all(slot_in, 'expert', split_axis=1, concat_axis=0, tiled=True)]
    all_to_all x2 -> x0, starting transfers between devices: 36.1 us -> none  [the longest x1 18.9 us: local(): lax.all_to_all(summed_dx, 'expert', split_axis=0, concat_axis=1, tiled=True)]
    dot_general x6 -> x0, matrix products: 21.5 us -> none  [the longest x1 4.44 us: local(): jnp.einsum('rkf,rkd->kfd', hidden_act, rows_grad, preferred_element_type=...]
    unnamed x12 -> x11, local copies, waits for them, and re-layouts: 1.93 us -> 8.42 us
  transfers between devices with their start and end apart: 6 -> 0, of which waited for: 5 -> 0; matrix products, arithmetic and copies ran while one was open for 7% -> 0% of each run, Pallas kernels for 0% -> 0%
where the time goes in v2:
time: 221 us; the launch traced here: 220 us
  Pallas kernels  190 us (86%)
  local copies, waits for them, and re-layouts  13.1 us (6%)
  matrix products  12.3 us (6%)
  other arithmetic  3.68 us (2%)
    pallas_call x1, Pallas kernels, expert_exchange(): pl.pallas_call(exchange_kernel, out_shape=(jax.ShapeDtypeStruct(pieces.sh...  165 us
    pallas_call x1, Pallas kernels, sum_over_devices(): pl.pallas_call(sum_kernel, out_shape=jax.ShapeDtypeStruct((GROUP,) + chun...  25.8 us
    unnamed x11, local copies, waits for them, and re-layouts  8.42 us

profile of v2, /device:TPU:1, one launch (start us, length us, event | category | flops | bytes accessed | tf_op | source)
XLA Modules:
  0.0 220.1 jit_solution(3090673053409179483)
XLA Ops:
  0.6 0.0 copy-start
  0.6 0.0 copy-start.1
  0.7 1.3 copy-done
  2.0 1.4 fusion.22
  3.3 0.7 fusion.32
  4.1 0.7 fusion.31
  4.7 0.3 convolution_convert_fusion
  5.0 0.1 stack.10
  5.1 0.2 copy.10
  5.3 0.4 convolution_convert_fusion.1
  5.6 0.1 stack.9
  5.7 0.2 copy.9
  5.9 0.4 maximum_bitcast_fusion
  6.3 0.8 reshape.45.pieces_ref
  7.2 3.7 %copy.11.w_in_ref = bf16[2,1280,320]{2,1,0:T(8,128)(2,1)} copy(bf16[2,1280,320]{1,2,0:T(8,128)(2,1)} %param.7) | data formatting | bytes 3276800 | tf_op args[2]
  10.8 164.6 %experts.1 = (bf16[16,16,640]{2,1,0:T(8,128)(2,1)}, bf16[2,1280,320]{2,1,0:T(8,128)(2,1)}, bf16[2,320,1280]{2,1,0:T(8,128)(2,1)}) custom-call(bf16[16,16,640]{2,1,0:T(8,128)(2,1)} %reshape.45.pieces_ref, bf16[2,1280,320]{2,1,0:T(8,128)(2,1)} %copy.11.w_in_ref, bf16[2,320,1280]{2,1,0:T(8,128)(2,1)} %w_out_ref.1), custom_call_target="tpu_custom_call" | custom-call | tf_op jit(solution)/shard_map/experts/pallas_call | solution.py:360
  175.4 1.1 reshape.46
  176.5 0.2 fusion.30
  176.7 0.1 copy.13
  176.9 0.1 unstack.15
  177.0 1.1 convolution_bitcast_fusion.1
  178.1 0.1 copy.12
  178.2 0.1 unstack.13
  178.3 0.5 convolution_bitcast_fusion
  178.8 1.9 fusion.13
  180.7 2.0 fusion.15
  182.6 25.8 %sum_keys.1 = f32[16,3,8,128]{3,2,1,0:T(8,128)} custom-call(f32[40,8,128]{2,1,0:T(8,128)} %bitcast.43), custom_call_target="tpu_custom_call" | custom-call | tf_op jit(solution)/shard_map/sum_keys/pallas_call | solution.py:96
  208.4 1.6 slice.6
  210.0 2.3 %copy.14 = bf16[2,1280,320]{1,2,0:T(8,128)(2,1)} copy(bf16[2,1280,320]{2,1,0:T(8,128)(2,1)S(1)} %copy-done.2) | data formatting | bytes 3276800
  212.3 3.1 %fusion.16 = f32[2,256,1280]{2,1,0:T(8,128)} fusion(f32[2,256,32]{1,2,0:T(8,128)} %fusion.13, f32[2,256,32]{1,2,0:T(8,128)} %convolution_bitcast_fusion.1, bf16[1280,32]{0,1:T(8,128)(2,1)} %param.6, f32[2,256,32]{1,2,0:T(8,128)} %get-tuple-element.17, f32[2,256]{1,0:T(2,128)S(1)} %get-tuple-element.16), kind=kOutput, calls=%fused_computation.21 | convolution fusion | flops 42058272 | bytes 2902016 | tf_op jit(solution)/shard_map/bps,ds->bpd/dot_general | solution.py:419
  215.4 3.6 %fusion.4 = bf16[2,256,1280]{2,1,0:T(8,128)(2,1)} fusion(f32[2,256,1280]{2,1,0:T(8,128)} %fusion.16, bf16[2,32,1280]{2,1,0:T(8,128)(2,1)S(1)} %unstack.13, f32[2,32]{1,0:T(2,128)S(1)} %get-tuple-element.18, f32[2,256,32]{1,2,0:T(8,128)S(1)} %fusion.22), kind=kOutput, calls=%fused_computation.5 | convolution fusion | flops 43303232 | bytes 4161792 | tf_op jit(solution)/shard_map/bps,bsd->bpd/dot_general | solution.py:418
  218.9 1.2 copy.16
  (5 shorter events, 0.0 us)
Async XLA Ops:
  0.6 1.3 copy-start
  0.6 4.1 %copy-start.1 = (bf16[2,256,1280]{2,1,0:T(8,128)(2,1)S(1)}, bf16[2,256,1280]{2,1,0:T(8,128)(2,1)}, u32[]{:S(2)}) copy-start(bf16[2,256,1280]{2,1,0:T(8,128)(2,1)} %param.9) | copy-start | bytes 3932164
  178.8 31.2 %copy-start.2 = (bf16[2,1280,320]{2,1,0:T(8,128)(2,1)S(1)}, bf16[2,1280,320]{2,1,0:T(8,128)(2,1)}, u32[]{:S(2)}) copy-start(bf16[2,1280,320]{2,1,0:T(8,128)(2,1)} %get-tuple-element.12) | copy-start | bytes 4915204
  215.4 3.6 %copy-start.3 = (bf16[2,320,1280]{2,1,0:T(8,128)(2,1)S(1)}, bf16[2,320,1280]{2,1,0:T(8,128)(2,1)}, u32[]{:S(2)}) copy-start(bf16[2,320,1280]{2,1,0:T(8,128)(2,1)} %get-tuple-element.27) | copy-start | bytes 4915204

commit v3 on v1

--- a/solution.py
+++ b/solution.py
@@ -7,20 +7,17 @@
 
 MESH = pl.DeviceIdType.MESH
 GROUP = 16
+Z, Y = 4, 4
+D = 1280
+HID = 320
+HALF = D // 2
+SIDE = 8
+SEEN = 16
+AWAY = (0, 1, 7, 2, 6, 3, 5, 4)
+PIECE = 16
 
 INV_ROOT2 = 0.7071067811865476
 INV_ROOT_TWO_PI = 0.3989422804014327
-
-
-def gelu_value(pre_act):
-    return 0.5 * pre_act * (1.0 + jax.scipy.special.erf(pre_act * INV_ROOT2))
-
-
-def gelu_slope(pre_act):
-    return (
-        0.5 * (1.0 + jax.scipy.special.erf(pre_act * INV_ROOT2))
-        + pre_act * jnp.exp(-0.5 * pre_act * pre_act) * INV_ROOT_TWO_PI
-    )
 
 
 def sum_kernel(x_ref, out_ref, src, landed_a, landed_b, part, total, send, recv):
@@ -119,6 +116,272 @@
     return out.reshape(3 * GROUP, 8, 128)[: x.shape[0]]
 
 
+def exchange_kernel(
+    pieces_ref, w_in_ref, w_out_ref,
+    back_ref, grad_in_ref, grad_out_ref,
+    landed, own, rows, part, hid, pre, from_left, from_right, sum_left, sum_right, sum_z, ready,
+    send_x, recv_x, send_b, recv_b, send_z, recv_z, send_s, recv_s,
+    send_y, recv_y, send_h, recv_h, send_f, recv_f, send_p, recv_p,
+):
+    row, col = lax.axis_index("dp"), lax.axis_index("expert")
+    yy = lax.rem(row, Y)
+    zz = lax.rem(col // 2, 2) * Z + row // Y
+    side = (col // 4) * 2 + lax.rem(col, 2)
+
+    def on_side(o):
+        p = lax.rem(side + o, SIDE)
+        return p, (row, (p // 2) * 4 + lax.rem(col // 2, 2) * 2 + lax.rem(p, 2))
+
+    def on_z(p):
+        return (lax.rem(p, Z) * Y + yy, (col // 4) * 4 + (p // Z) * 2 + lax.rem(col, 2))
+
+    def on_y(o):
+        return ((row // Y) * Y + lax.rem(yy + o + Y, Y), col)
+
+    right, left = on_y(1), on_y(-1)
+
+    def remote(src, dst, send, recv, device):
+        return pltpu.make_async_remote_copy(
+            src_ref=src, dst_ref=dst, send_sem=send, recv_sem=recv,
+            device_id=device, device_id_type=MESH,
+        )
+
+    barrier = pltpu.get_barrier_semaphore()
+    for o in range(1, SIDE):
+        pl.semaphore_signal(barrier, inc=1, device_id=on_side(o)[1], device_id_type=MESH)
+        pl.semaphore_signal(
+            barrier, inc=1, device_id=on_z(lax.rem(zz + o, 2 * Z)), device_id_type=MESH
+        )
+    pl.semaphore_signal(barrier, inc=1, device_id=right, device_id_type=MESH)
+    pl.semaphore_signal(barrier, inc=1, device_id=left, device_id_type=MESH)
+    pl.semaphore_wait(barrier, 2 * (SIDE - 1) + 2)
+
+    def piece_out(o):
+        p, there = on_side(o)
+        return remote(pieces_ref.at[p], landed.at[side], send_x.at[o], recv_x.at[o], there)
+
+    for o in range(1, SIDE):
+        piece_out(o).start()
+    landed[side] = pieces_ref[side]
+
+    size = SIDE * PIECE
+    r = lax.broadcasted_iota(jnp.int32, (size, size), 0)
+    c = lax.broadcasted_iota(jnp.int32, (size, size), 1)
+    turn = (c == ((r >> 1) & 7) * 16 + (r >> 4) * 2 + (r & 1)).astype(jnp.bfloat16)
+
+    def turned(x):
+        return jnp.dot(turn, x, preferred_element_type=jnp.float32).astype(jnp.bfloat16)
+
+    parts_of_piece = [(h, t, s) for h in range(2) for t in range(2) for s in range(2)]
+    for o in range(1, SIDE):
+        piece_out(o).wait_recv()
+    for g in range(2):
+        block = turned(landed[:, g].reshape(size, HALF))
+        for k, (h, t, s) in enumerate(parts_of_piece):
+            own[g, t, s, :, h * HALF : (h + 1) * HALF] = block[k * SEEN : (k + 1) * SEEN]
+
+    def place(q):
+        return lax.rem(zz - AWAY[q] + 2 * Z, 2 * Z)
+
+    def along_z(q):
+        p = lax.rem(zz + AWAY[q], 2 * Z)
+        return remote(own.at[p // Z], rows.at[zz, yy], send_z.at[q], recv_z.at[q], on_z(p))
+
+    def along_y(q, d):
+        mine = rows.at[place(q), yy]
+        return remote(mine, mine, send_y.at[q, d], recv_y.at[q, d], left if d else right)
+
+    def onward(q, d):
+        ours = rows.at[place(q), lax.rem(yy + (1 if d else Y - 1), Y), d]
+        return remote(ours, ours, send_h.at[q, d], recv_h.at[q, d], left if d else right)
+
+    def times(a, b, over):
+        return lax.dot_general(a, b, (over, ((), ())), preferred_element_type=jnp.float32)
+
+    def experts(q):
+        p = place(q)
+        for s in range(2):
+            x = rows[p, :, 0, s].reshape(Y * SEEN, D)
+            g = rows[p, :, 1, s].reshape(Y * SEEN, D)
+            pre_act = times(x, w_in_ref[s], ((1,), (1,)))
+            act_grad = times(g, w_out_ref[s], ((1,), (1,)))
+            cdf = 0.5 * (1.0 + lax.erf(pre_act * INV_ROOT2))
+            hidden = (pre_act * cdf).astype(jnp.bfloat16)
+            slope = cdf + pre_act * jnp.exp(-0.5 * pre_act * pre_act) * INV_ROOT_TWO_PI
+            pre_grad = (act_grad * slope).astype(jnp.bfloat16)
+            hid[s, p] = hidden
+            pre[s, p] = pre_grad
+            out = times(hidden, w_out_ref[s], ((1,), (0,)))
+            part[p, :, 0, s] = out.astype(jnp.bfloat16).reshape(Y, SEEN, D)
+            back = times(pre_grad, w_in_ref[s], ((1,), (0,)))
+            part[p, :, 1, s] = back.astype(jnp.bfloat16).reshape(Y, SEEN, D)
+
+    def far(q, d):
+        ours = part.at[place(q), lax.rem(yy + 2, Y), d]
+        land = (from_right if d else from_left).at[q]
+        return remote(ours, land, send_f.at[q, d], recv_f.at[q, d], left if d else right)
+
+    def near(q, d):
+        ours = part.at[place(q), lax.rem(yy + (Y - 1 if d else 1), Y)]
+        land = (sum_right if d else sum_left).at[q]
+        return remote(ours, land, send_p.at[q, d], recv_p.at[q, d], left if d else right)
+
+    def along_z_back(q):
+        p = place(q)
+        return remote(part.at[p, yy], sum_z.at[zz], send_s.at[q], recv_s.at[q], on_z(p))
+
+    def begin(q):
+        for d in range(2):
+            far(q, d).start()
+
+    def pass_on(q):
+        for d in range(2):
+            far(q, d).wait_recv()
+            ours = part.at[place(q), lax.rem(yy + (Y - 1 if d else 1), Y), d]
+            other = (from_right if d else from_left)[q].astype(jnp.float32)
+            ours[...] = (ours[...].astype(jnp.float32) + other).astype(jnp.bfloat16)
+            near(q, d).start()
+
+    def collect(q):
+        for d in range(2):
+            near(q, d).wait_recv()
+        total = (
+            part[place(q), yy].astype(jnp.float32)
+            + sum_left[q].astype(jnp.float32)
+            + sum_right[q].astype(jnp.float32)
+        ).astype(jnp.bfloat16)
+        if q == 0:
+            sum_z[zz] = total
+        else:
+            part[place(q), yy] = total
+            along_z_back(q).start()
+
+    last = len(AWAY) - 1
+    for q in range(1, 4):
+        along_z(q).start()
+    rows[zz, yy] = own[zz // Z]
+
+    def fetch(q):
+        if 1 <= q <= last:
+            along_z(q).wait_recv()
+            if q + 3 <= last:
+                along_z(q + 3).start()
+        if q <= last:
+            for d in range(2):
+                along_y(q, d).start()
+
+    def spread(q):
+        if q <= last:
+            for d in range(2):
+                along_y(q, d).wait_recv()
+                onward(q, d).start()
+
+    fetch(0)
+    fetch(1)
+    spread(0)
+    for q in range(last + 1):
+        fetch(q + 2)
+        spread(q + 1)
+        for d in range(2):
+            onward(q, d).wait_recv()
+        experts(q)
+        if q >= 1:
+            begin(q)
+        if q >= 2:
+            pass_on(q - 1)
+        if q >= 3:
+            collect(q - 2)
+    begin(0)
+
+    for s in range(2):
+        p_all = pre[s].reshape(2 * Z * Y * SEEN, HID)
+        h_all = hid[s].reshape(2 * Z * Y * SEEN, HID)
+        for k in range(0, D, 256):
+            x = rows[:, :, 0, s, :, k : k + 256].reshape(2 * Z * Y * SEEN, 256)
+            g = rows[:, :, 1, s, :, k : k + 256].reshape(2 * Z * Y * SEEN, 256)
+            grad_in_ref[s, :, k : k + 256] = times(p_all, x, ((0,), (0,))).astype(jnp.bfloat16)
+            grad_out_ref[s, :, k : k + 256] = times(h_all, g, ((0,), (0,))).astype(jnp.bfloat16)
+        if s == 0:
+            pass_on(last)
+            collect(last - 1)
+            pass_on(0)
+    collect(last)
+    collect(0)
+
+    for q in range(1, last + 1):
+        along_z_back(q).wait_recv()
+    for g in range(2):
+        total = sum_z[g * Z].astype(jnp.float32)
+        for k in range(1, Z):
+            total = total + sum_z[g * Z + k].astype(jnp.float32)
+        total = total.astype(jnp.bfloat16)
+        stack = jnp.concatenate(
+            [total[t, s, :, h * HALF : (h + 1) * HALF] for h, t, s in parts_of_piece], axis=0
+        )
+        ready[:, g] = turned(stack).reshape(SIDE, PIECE, HALF)
+
+    def piece_back(o):
+        p, there = on_side(o)
+        return remote(ready.at[p], back_ref.at[side], send_b.at[o], recv_b.at[o], there)
+
+    for o in range(1, SIDE):
+        piece_back(o).start()
+    back_ref[side] = ready[side]
+    for o in range(1, SIDE):
+        piece_back(o).wait_recv()
+
+    for o in range(1, SIDE):
+        piece_out(o).wait_send()
+        piece_back(o).wait_send()
+    for q in range(last + 1):
+        if q > 0:
+            along_z(q).wait_send()
+            along_z_back(q).wait_send()
+        for d in range(2):
+            along_y(q, d).wait_send()
+            onward(q, d).wait_send()
+            far(q, d).wait_send()
+            near(q, d).wait_send()
+
+
+def expert_exchange(pieces, w_in_turned, w_out):
+    block = (2, 2, SEEN, D)
+    slabs = 2 * Z
+    bf16 = jnp.bfloat16
+    dma = pltpu.SemaphoreType.DMA
+    vmem = pl.BlockSpec(memory_space=pltpu.VMEM)
+    return pl.pallas_call(
+        exchange_kernel,
+        out_shape=(
+            jax.ShapeDtypeStruct(pieces.shape, bf16),
+            jax.ShapeDtypeStruct(w_out.shape, bf16),
+            jax.ShapeDtypeStruct(w_out.shape, bf16),
+        ),
+        in_specs=[vmem] * 3,
+        out_specs=(vmem,) * 3,
+        scratch_shapes=[
+            pltpu.VMEM(pieces.shape, bf16),
+            pltpu.VMEM((2,) + block, bf16),
+            pltpu.VMEM((slabs, Y) + block, bf16),
+            pltpu.VMEM((slabs, Y) + block, bf16),
+            pltpu.VMEM((2, slabs, Y * SEEN, HID), bf16),
+            pltpu.VMEM((2, slabs, Y * SEEN, HID), bf16),
+            pltpu.VMEM((slabs,) + block[1:], bf16),
+            pltpu.VMEM((slabs,) + block[1:], bf16),
+            pltpu.VMEM((slabs,) + block, bf16),
+            pltpu.VMEM((slabs,) + block, bf16),
+            pltpu.VMEM((slabs,) + block, bf16),
+            pltpu.VMEM(pieces.shape, bf16),
+        ]
+        + [dma((SIDE,))] * 8
+        + [dma((slabs, 2))] * 8,
+        compiler_params=pltpu.CompilerParams(
+            collective_id=0, has_side_effects=True, vmem_limit_bytes=56 * 1024 * 1024
+        ),
+        name="experts",
+    )(pieces, w_in_turned, w_out)
+
+
 def local(tokens, slot_keys, w_in, w_out, grad_out):
     logits = jnp.einsum("bpd,ds->bps", tokens, slot_keys, preferred_element_type=jnp.float32)
     dispatch = jax.nn.softmax(logits, axis=1)
@@ -131,42 +394,14 @@
     slot_grad = jnp.einsum(
         "bps,bpd->bsd", combine_low, grad_out, preferred_element_type=jnp.float32
     ).astype(jnp.bfloat16)
-    sent_in, sent_grad = (
-        lax.all_to_all(slot_in, "expert", split_axis=1, concat_axis=0, tiled=True),
-        lax.all_to_all(slot_grad, "expert", split_axis=1, concat_axis=0, tiled=True),
-    )
-    rows_in, rows_grad = (
-        lax.all_gather(sent_in, "dp", axis=0, tiled=True),
-        lax.all_gather(sent_grad, "dp", axis=0, tiled=True),
-    )
-    pre_act = jnp.einsum("rkd,kdf->rkf", rows_in, w_in, preferred_element_type=jnp.float32)
-    hidden_act = gelu_value(pre_act).astype(jnp.bfloat16)
-    act_grad = jnp.einsum("rkd,kfd->rkf", rows_grad, w_out, preferred_element_type=jnp.float32)
-    pre_grad = (act_grad * gelu_slope(pre_act)).astype(jnp.bfloat16)
-    grad_w_out = jnp.einsum(
-        "rkf,rkd->kfd", hidden_act, rows_grad, preferred_element_type=jnp.float32
-    ).astype(jnp.bfloat16)
-    grad_w_in = jnp.einsum(
-        "rkd,rkf->kdf", rows_in, pre_grad, preferred_element_type=jnp.float32
-    ).astype(jnp.bfloat16)
-    summed_out = lax.psum_scatter(
-        jnp.einsum("rkf,kfd->rkd", hidden_act, w_out, preferred_element_type=jnp.float32).astype(
-            jnp.bfloat16
-        ),
-        "dp",
-        scatter_dimension=0,
-        tiled=True,
-    )
-    slot_out = lax.all_to_all(summed_out, "expert", split_axis=0, concat_axis=1, tiled=True)
-    summed_dx = lax.psum_scatter(
-        jnp.einsum("rkf,kdf->rkd", pre_grad, w_in, preferred_element_type=jnp.float32).astype(
-            jnp.bfloat16
-        ),
-        "dp",
-        scatter_dimension=0,
-        tiled=True,
-    )
-    slot_dx = lax.all_to_all(summed_dx, "expert", split_axis=0, concat_axis=1, tiled=True)
+    images, slots, width = slot_in.shape
+    pieces = jnp.stack([slot_in, slot_grad]).reshape(2, images, 4, 2, 2, slots // GROUP, 2, HALF)
+    pieces = pieces.transpose(2, 4, 3, 6, 0, 5, 1, 7).reshape(SIDE, 2, PIECE, HALF)
+    back, grad_w_in, grad_w_out = expert_exchange(pieces, w_in.transpose(0, 2, 1), w_out)
+    grad_w_in = grad_w_in.transpose(0, 2, 1)
+    back = back.reshape(4, 2, 2, 2, 2, slots // GROUP, images, HALF)
+    back = back.transpose(4, 6, 0, 2, 1, 5, 3, 7)
+    slot_out, slot_dx = back.reshape(2, images, slots, width)
     comb_grad = jnp.einsum("bpd,bsd->bps", grad_out, slot_out, preferred_element_type=jnp.float32)
     comb_logit = combine * (comb_grad - jnp.sum(combine * comb_grad, axis=2, keepdims=True))
     disp_grad = jnp.einsum("bpd,bsd->bps", tokens, slot_dx, preferred_element_type=jnp.float32)
@@ -177,7 +412,6 @@
         + jnp.einsum("bps,ds->bpd", logit_grad, slot_keys, preferred_element_type=jnp.float32)
     ).astype(jnp.bfloat16)
     key_terms = jnp.einsum("bpd,bps->sd", tokens, logit_grad, preferred_element_type=jnp.float32)
-    slots, width = key_terms.shape
     tiles = key_terms.reshape(slots // 8, 8, width // 128, 128).transpose(0, 2, 1, 3)
     summed = sum_over_devices(tiles.reshape(-1, 8, 128))
     summed = summed.reshape(slots // 8, width // 128, 8, 128).transpose(0, 2, 1, 3)

time: 447 us -> 175 us (0.39)
  waiting for transfers between devices: 285 us -> 0 us
  Pallas kernels: 25.4 us -> 154 us
  starting transfers between devices: 36.3 us -> 0 us
  blocking collectives: 36.2 us -> 0 us
  matrix products: 36.7 us -> 9.6 us
  between operations: 13.9 us -> 0.77 us
    reduce_scatter x2 -> x0, waiting for transfers between devices: 147 us -> none  [the longest x1 82.5 us: local(): lax.psum_scatter(jnp.einsum('rkf,kfd->rkd', hidden_act, w_out, preferred_...]
    all_gather x2 -> x0, waiting for transfers between devices: 135 us -> none  [the longest x1 78.5 us: local(): lax.all_gather(sent_grad, 'dp', axis=0, tiled=True)]
    pallas_call x0 -> x1, Pallas kernels: none -> 128 us  [expert_exchange(): pl.pallas_call(exchange_kernel, out_shape=(jax.ShapeDtypeStruct(pieces.sh...]
    all_to_all x2 -> x0, blocking collectives: 36.2 us -> none  [the longest x1 22.7 us: local(): lax.all_to_all(slot_in, 'expert', split_axis=1, concat_axis=0, tiled=True)]
    all_to_all x2 -> x0, starting transfers between devices: 36.1 us -> none  [the longest x1 18.9 us: local(): lax.all_to_all(summed_dx, 'expert', split_axis=0, concat_axis=1, tiled=True)]
    dot_general x6 -> x0, matrix products: 21.5 us -> none  [the longest x1 4.44 us: local(): jnp.einsum('rkf,rkd->kfd', hidden_act, rows_grad, preferred_element_type=...]
  transfers between devices with their start and end apart: 6 -> 0, of which waited for: 5 -> 0; matrix products, arithmetic and copies ran while one was open for 7% -> 0% of each run, Pallas kernels for 0% -> 0%
where the time goes in v3:
time: 175 us
  Pallas kernels  154 us (88%)
  matrix products  9.6 us (5%)
  local copies, waits for them, and re-layouts  9.21 us (5%)
    pallas_call x1, Pallas kernels, expert_exchange(): pl.pallas_call(exchange_kernel, out_shape=(jax.ShapeDtypeStruct(pieces.sh...  128 us
    pallas_call x1, Pallas kernels, sum_over_devices(): pl.pallas_call(sum_kernel, out_shape=jax.ShapeDtypeStruct((GROUP,) + chun...  26.2 us
    unnamed x12, local copies, waits for them, and re-layouts  4.5 us
    dot_general x1, matrix products, local(): jnp.einsum('bps,bsd->bpd', dispatch_low, slot_dx, preferred_element_type=...  3.56 us

profile of v3, /device:TPU:1, one launch (start us, length us, event | category | flops | bytes accessed | tf_op | source)
XLA Modules:
  0.0 174.6 jit_solution(5464655108890941185)
XLA Ops:
  0.6 0.0 copy-start
  0.6 0.0 copy-start.1
  0.7 1.3 copy-done
  2.0 1.4 fusion.22
  3.3 0.4 fusion.32
  3.7 0.2 fusion.31
  3.8 0.3 convolution_convert_fusion
  4.2 0.1 stack.10
  4.2 0.2 copy.10
  4.4 0.4 convolution_convert_fusion.1
  4.8 0.1 stack.9
  4.8 0.2 copy.9
  5.0 0.4 maximum_bitcast_fusion
  5.4 0.8 reshape.45.pieces_ref
  6.3 127.6 %experts.1 = (bf16[8,2,16,640]{3,2,1,0:T(8,128)(2,1)}, bf16[2,320,1280]{2,1,0:T(8,128)(2,1)}, bf16[2,320,1280]{2,1,0:T(8,128)(2,1)}) custom-call(bf16[8,2,16,640]{3,2,1,0:T(8,128)(2,1)} %reshape.45.pieces_ref, bf16[2,320,1280]{2,1,0:T(8,128)(2,1)} %bitcast.45, bf16[2,320,1280]{2,1,0:T(8,128)(2,1)} %w_out_ref.1), custom_call_target="tpu_custom_call" | custom-call | tf_op jit(solution)/shard_map/experts/pallas_call | solution.py:353
  133.9 1.1 reshape.46
  135.0 0.2 fusion.30
  135.2 0.1 copy.12
  135.4 0.1 unstack.15
  135.5 0.5 convolution_bitcast_fusion.1
  135.9 0.1 copy.11
  136.1 0.1 unstack.13
  136.2 0.5 convolution_bitcast_fusion
  136.7 0.3 fusion.13
  137.0 1.0 fusion.15
  138.0 26.2 %sum_keys.1 = f32[16,3,8,128]{3,2,1,0:T(8,128)} custom-call(f32[40,8,128]{2,1,0:T(8,128)} %bitcast.49), custom_call_target="tpu_custom_call" | custom-call | tf_op jit(solution)/shard_map/sum_keys/pallas_call | solution.py:99
  164.2 1.6 slice.6
  165.8 2.1 %fusion.16 = f32[2,256,1280]{2,1,0:T(8,128)} fusion(f32[2,256,32]{1,2,0:T(8,128)S(1)} %fusion.13, f32[2,256,32]{1,2,0:T(8,128)S(1)} %convolution_bitcast_fusion.1, bf16[1280,32]{0,1:T(8,128)(2,1)S(1)} %copy-done.4, f32[2,256,32]{1,2,0:T(8,128)S(1)} %get-tuple-element.13, f32[2,256]{1,0:T(2,128)S(1)} %get-tuple-element.12), kind=kOutput, calls=%fused_computation.21 | convolution fusion | flops 42058272 | bytes 2902016 | tf_op jit(solution)/shard_map/bps,ds->bpd/dot_general | solution.py:412
  167.9 3.6 %fusion.4 = bf16[2,256,1280]{2,1,0:T(8,128)(2,1)} fusion(f32[2,256,1280]{2,1,0:T(8,128)} %fusion.16, bf16[2,32,1280]{2,1,0:T(8,128)(2,1)S(1)} %unstack.13, f32[2,32]{1,0:T(2,128)S(1)} %get-tuple-element.14, f32[2,256,32]{1,2,0:T(8,128)S(1)} %fusion.22), kind=kOutput, calls=%fused_computation.5 | convolution fusion | flops 43303232 | bytes 4161792 | tf_op jit(solution)/shard_map/bps,bsd->bpd/dot_general | solution.py:411
  171.4 1.2 copy.15
  172.6 0.9 copy-done.2
  173.4 1.2 copy.16
  (6 shorter events, 0.0 us)
Async XLA Ops:
  0.6 1.3 copy-start
  0.6 3.2 %copy-start.1 = (bf16[2,256,1280]{2,1,0:T(8,128)(2,1)S(1)}, bf16[2,256,1280]{2,1,0:T(8,128)(2,1)}, u32[]{:S(2)}) copy-start(bf16[2,256,1280]{2,1,0:T(8,128)(2,1)} %param.9) | copy-start | bytes 3932164
  136.7 29.1 %copy-start.4 = (bf16[1280,32]{0,1:T(8,128)(2,1)S(1)}, bf16[1280,32]{0,1:T(8,128)(2,1)}, u32[]{:S(2)}) copy-start(bf16[1280,32]{0,1:T(8,128)(2,1)} %param.6) | copy-start | bytes 245764
  167.9 3.6 %copy-start.3 = (bf16[2,320,1280]{2,1,0:T(8,128)(2,1)S(1)}, bf16[2,320,1280]{2,1,0:T(8,128)(2,1)}, u32[]{:S(2)}) copy-start(bf16[2,320,1280]{2,1,0:T(8,128)(2,1)} %get-tuple-element.8) | copy-start | bytes 4915204
  171.4 2.0 %copy-start.2 = (bf16[2,320,1280]{2,1,0:T(8,128)(2,1)S(1)}, bf16[2,320,1280]{2,1,0:T(8,128)(2,1)}, u32[]{:S(2)}) copy-start(bf16[2,320,1280]{2,1,0:T(8,128)(2,1)} %get-tuple-element.23) | copy-start | bytes 4915204

commit v4 on v3

--- a/solution.py
+++ b/solution.py
@@ -11,6 +11,8 @@
 D = 1280
 HID = 320
 HALF = D // 2
+SLOTS = 32
+TILES = D // 128
 SIDE = 8
 SEEN = 16
 AWAY = (0, 1, 7, 2, 6, 3, 5, 4)
@@ -20,100 +22,206 @@
 INV_ROOT_TWO_PI = 0.3989422804014327
 
 
-def sum_kernel(x_ref, out_ref, src, landed_a, landed_b, part, total, send, recv):
+def times(a, b, over):
+    return lax.dot_general(a, b, (over, ((), ())), preferred_element_type=jnp.float32)
+
+
+def soft(x, axis):
+    e = jnp.exp(x - jnp.max(x, axis=axis, keepdims=True))
+    return e / jnp.sum(e, axis=axis, keepdims=True)
+
+
+def combine_kernel(
+    tokens_ref, grad_ref, keys_ref, back_ref, dx_ref, keys_out_ref,
+    terms, other, chunks, landed, part, parts_z, total, done, done_other,
+    send_c, recv_c, send_a, recv_a, send_z, recv_z, send_d, recv_d,
+):
     row, col = lax.axis_index("dp"), lax.axis_index("expert")
-
-    def at(axis, offset):
-        if axis == 0:
-            return (lax.rem(row + offset, GROUP), col)
-        return (row, lax.rem(col + offset, GROUP))
+    xx, yy, core = col // 4, lax.rem(row, Y), lax.rem(col, 2)
+    half_z = lax.rem(col // 2, 2)
+    zz = half_z * Z + row // Y
+    flat = xx * Y + yy
+
+    def on_plane(p):
+        return ((row // Y) * Y + lax.rem(p, Y), (p // Y) * 4 + half_z * 2 + core)
+
+    def on_z(p):
+        return (lax.rem(p, Z) * Y + yy, xx * 4 + (p // Z) * 2 + core)
+
+    twin = (row, col - core + 1 - core)
+
+    def remote(src, dst, send, recv, device):
+        return pltpu.make_async_remote_copy(
+            src_ref=src, dst_ref=dst, send_sem=send, recv_sem=recv,
+            device_id=device, device_id_type=MESH,
+        )
 
     barrier = pltpu.get_barrier_semaphore()
-
-    @pl.loop(1, GROUP)
-    def _(o):
-        for axis in range(2):
-            pl.semaphore_signal(barrier, inc=1, device_id=at(axis, o), device_id_type=MESH)
-
-    tiles = x_ref.shape[0]
-    src[pl.ds(0, tiles)] = x_ref[...]
-    src[pl.ds(tiles, src.shape[0] - tiles)] = jnp.zeros(
-        (src.shape[0] - tiles,) + src.shape[1:], src.dtype
-    )
-    pl.semaphore_wait(barrier, 2 * (GROUP - 1))
-
-    def copy(round_, o):
-        if round_ == 0:
-            there = at(0, o)
-            a, b = src.at[pl.ds(3 * there[0], 3)], landed_a.at[o]
-        elif round_ == 1:
-            there = at(1, o)
-            a, b = part, landed_b.at[o]
-        else:
-            there = at(0, o)
-            a, b = total, out_ref.at[row]
-        return pltpu.make_async_remote_copy(
-            src_ref=a,
-            dst_ref=b,
-            send_sem=send.at[round_, o],
-            recv_sem=recv.at[round_, o],
-            device_id=there,
-            device_id_type=MESH,
+    pl.semaphore_signal(barrier, inc=1, device_id=twin, device_id_type=MESH)
+    for o in range(1, GROUP):
+        p = lax.rem(flat + o, GROUP)
+        pl.semaphore_signal(barrier, inc=1, device_id=on_plane(p), device_id_type=MESH)
+    for o in range(1, 2 * Z):
+        p = lax.rem(zz + o, 2 * Z)
+        pl.semaphore_signal(barrier, inc=1, device_id=on_z(p), device_id_type=MESH)
+
+    size = GROUP * PIECE
+    r = lax.broadcasted_iota(jnp.int32, (size, size), 0)
+    c = lax.broadcasted_iota(jnp.int32, (size, size), 1)
+    home = ((r >> 3) & 3) * 64 + ((r >> 1) & 1) * 32 + ((r >> 2) & 1) * 16
+    home = home + (r >> 7) * 8 + ((r >> 6) & 1) * 4 + (r & 1) * 2 + ((r >> 5) & 1)
+    turn = (c == home).astype(jnp.bfloat16)
+    slots = times(turn, back_ref[...].reshape(size, HALF), ((1,), (0,))).astype(jnp.bfloat16)
+
+    def slot_rows(t, i):
+        k = (t * 2 + i) * SLOTS
+        return jnp.concatenate(
+            [slots[h * 4 * SLOTS + k : h * 4 * SLOTS + k + SLOTS] for h in range(2)], axis=1
         )
 
-    def start(round_):
-        @pl.loop(1, GROUP)
-        def _(o):
-            copy(round_, o).start()
-
-    def finish(round_):
-        @pl.loop(1, GROUP)
-        def _(o):
-            copy(round_, o).wait_recv()
-
-    start(0)
-    finish(0)
-    acc = src[pl.ds(3 * row, 3)]
+    keys = keys_ref[...]
+    weights, sums = [], None
+    for i in range(2):
+        slot_out, slot_dx = slot_rows(0, i), slot_rows(1, i)
+        both = times(jnp.concatenate([keys, slot_dx], axis=0), tokens_ref[i], ((1,), (1,)))
+        logits, disp_grad = both[:SLOTS], both[SLOTS:]
+        dispatch, combine = soft(logits, 1), soft(logits, 0)
+        comb_grad = times(slot_out, grad_ref[i], ((1,), (1,)))
+        inner = jnp.sum(combine * comb_grad, axis=0, keepdims=True)
+        comb_logit = combine * (comb_grad - inner)
+        inner = jnp.sum(dispatch * disp_grad, axis=1, keepdims=True)
+        disp_logit = dispatch * (disp_grad - inner)
+        logit_grad = (comb_logit + disp_logit).astype(jnp.bfloat16)
+        term = times(logit_grad, tokens_ref[i], ((1,), (0,)))
+        sums = term if sums is None else sums + term
+        weights.append(
+            (
+                jnp.concatenate([dispatch.astype(jnp.bfloat16), logit_grad], axis=0),
+                jnp.concatenate([slot_dx, keys], axis=0),
+            )
+        )
+
+    def token_grads(i):
+        a, b = weights[i]
+        dx_ref[i] = times(a, b, ((0,), (0,))).astype(jnp.bfloat16)
+
+    for h in range(2):
+        terms[h] = sums[h * SLOTS // 2 : (h + 1) * SLOTS // 2]
+    pl.semaphore_wait(barrier, 1 + GROUP - 1 + 2 * Z - 1)
+    to_twin = remote(terms.at[1 - core], other, send_c.at[0], recv_c.at[0], twin)
+    to_twin.start()
+    token_grads(0)
+    to_twin.wait_recv()
+    mine = terms[core] + other[...]
+    for k in range(TILES):
+        chunks[k] = mine[:, k * 128 : (k + 1) * 128]
+
+    def to_owner(o):
+        p = lax.rem(flat + o, GROUP)
+        return remote(chunks.at[p], landed.at[o], send_a.at[o], recv_a.at[o], on_plane(p))
+
+    def from_owner(o):
+        p = lax.rem(flat + o, GROUP)
+        return remote(total, done.at[flat], send_d.at[o], recv_d.at[o], on_plane(p))
+
+    def across_z(o):
+        p = lax.rem(zz + o, 2 * Z)
+        return remote(part, parts_z.at[zz], send_z.at[o], recv_z.at[o], on_z(p))
+
+    owner = flat < TILES
     for o in range(1, GROUP):
-        acc = acc + landed_a[o]
-    part[...] = acc
-    start(1)
-    finish(1)
-    acc = jnp.zeros(part.shape, part.dtype)
-    landed_b[0] = part[...]
-    for c in range(GROUP):
-        acc = acc + landed_b[lax.rem(col - c + GROUP, GROUP)]
-    total[...] = acc
-    start(2)
-    out_ref[row] = acc
-    finish(2)
-
-    @pl.loop(1, GROUP)
-    def _(o):
-        for r in range(3):
-            copy(r, o).wait_send()
-
-
-def sum_over_devices(x):
-    chunk = (3, 8, 128)
-    out = pl.pallas_call(
-        sum_kernel,
-        out_shape=jax.ShapeDtypeStruct((GROUP,) + chunk, jnp.float32),
-        in_specs=[pl.BlockSpec(memory_space=pltpu.VMEM)],
-        out_specs=pl.BlockSpec(memory_space=pltpu.VMEM),
+
+        @pl.when(lax.rem(flat + o, GROUP) < TILES)
+        def _():
+            to_owner(o).start()
+
+    token_grads(1)
+
+    @pl.when(owner)
+    def _():
+        acc = chunks[flat]
+        for o in range(1, GROUP):
+            to_owner(o).wait_recv()
+            acc = acc + landed[o]
+        part[...] = acc
+        for o in range(1, 2 * Z):
+            across_z(o).start()
+        parts_z[zz] = acc
+        for o in range(1, 2 * Z):
+            across_z(o).wait_recv()
+        acc = parts_z[0]
+        for k in range(1, 2 * Z):
+            acc = acc + parts_z[k]
+        total[...] = acc
+        for o in range(1, GROUP):
+            from_owner(o).start()
+        done[flat] = acc
+
+    for o in range(1, GROUP):
+
+        @pl.when(lax.rem(flat - o + GROUP, GROUP) < TILES)
+        def _():
+            from_owner(o).wait_recv()
+
+    back_to_twin = remote(done.at[pl.ds(0, TILES)], done_other, send_c.at[1], recv_c.at[1], twin)
+    back_to_twin.start()
+    first = pl.ds(pl.multiple_of(core * (SLOTS // 2), SLOTS // 2), SLOTS // 2)
+    second = pl.ds(pl.multiple_of((1 - core) * (SLOTS // 2), SLOTS // 2), SLOTS // 2)
+    for k in range(TILES):
+        keys_out_ref[first, k * 128 : (k + 1) * 128] = done[k]
+    back_to_twin.wait_recv()
+    for k in range(TILES):
+        keys_out_ref[second, k * 128 : (k + 1) * 128] = done_other[k]
+
+    to_twin.wait_send()
+    back_to_twin.wait_send()
+    for o in range(1, GROUP):
+
+        @pl.when(lax.rem(flat + o, GROUP) < TILES)
+        def _():
+            to_owner(o).wait_send()
+
+    @pl.when(owner)
+    def _():
+        for o in range(1, GROUP):
+            from_owner(o).wait_send()
+        for o in range(1, 2 * Z):
+            across_z(o).wait_send()
+
+
+def combine_gradients(tokens, grad_out, keys_turned, back):
+    f32 = jnp.float32
+    dma = pltpu.SemaphoreType.DMA
+    vmem = pl.BlockSpec(memory_space=pltpu.VMEM)
+    tile = (SLOTS // 2, 128)
+    return pl.pallas_call(
+        combine_kernel,
+        out_shape=(
+            jax.ShapeDtypeStruct(tokens.shape, jnp.bfloat16),
+            jax.ShapeDtypeStruct(keys_turned.shape, f32),
+        ),
+        in_specs=[vmem] * 4,
+        out_specs=(vmem,) * 2,
         scratch_shapes=[
-            pltpu.VMEM((3 * GROUP, 8, 128), jnp.float32),
-            pltpu.VMEM((GROUP,) + chunk, jnp.float32),
-            pltpu.VMEM((GROUP,) + chunk, jnp.float32),
-            pltpu.VMEM(chunk, jnp.float32),
-            pltpu.VMEM(chunk, jnp.float32),
-            pltpu.SemaphoreType.DMA((3, GROUP)),
-            pltpu.SemaphoreType.DMA((3, GROUP)),
+            pltpu.VMEM((2, SLOTS // 2, D), f32),
+            pltpu.VMEM((SLOTS // 2, D), f32),
+            pltpu.VMEM((GROUP,) + tile, f32),
+            pltpu.VMEM((GROUP,) + tile, f32),
+            pltpu.VMEM(tile, f32),
+            pltpu.VMEM((2 * Z,) + tile, f32),
+            pltpu.VMEM(tile, f32),
+            pltpu.VMEM((GROUP,) + tile, f32),
+            pltpu.VMEM((TILES,) + tile, f32),
+            dma((2,)), dma((2,)),
+            dma((GROUP,)), dma((GROUP,)),
+            dma((2 * Z,)), dma((2 * Z,)),
+            dma((GROUP,)), dma((GROUP,)),
         ],
-        compiler_params=pltpu.CompilerParams(collective_id=1, has_side_effects=True),
-        name="sum_keys",
-    )(x)
-    return out.reshape(3 * GROUP, 8, 128)[: x.shape[0]]
+        compiler_params=pltpu.CompilerParams(
+            collective_id=1, has_side_effects=True, vmem_limit_bytes=48 * 1024 * 1024
+        ),
+        name="combine",
+    )(tokens, grad_out, keys_turned, back)
 
 
 def exchange_kernel(
@@ -194,9 +302,6 @@
     def onward(q, d):
         ours = rows.at[place(q), lax.rem(yy + (1 if d else Y - 1), Y), d]
         return remote(ours, ours, send_h.at[q, d], recv_h.at[q, d], left if d else right)
-
-    def times(a, b, over):
-        return lax.dot_general(a, b, (over, ((), ())), preferred_element_type=jnp.float32)
 
     def experts(q):
         p = place(q)
@@ -399,24 +504,8 @@
     pieces = pieces.transpose(2, 4, 3, 6, 0, 5, 1, 7).reshape(SIDE, 2, PIECE, HALF)
     back, grad_w_in, grad_w_out = expert_exchange(pieces, w_in.transpose(0, 2, 1), w_out)
     grad_w_in = grad_w_in.transpose(0, 2, 1)
-    back = back.reshape(4, 2, 2, 2, 2, slots // GROUP, images, HALF)
-    back = back.transpose(4, 6, 0, 2, 1, 5, 3, 7)
-    slot_out, slot_dx = back.reshape(2, images, slots, width)
-    comb_grad = jnp.einsum("bpd,bsd->bps", grad_out, slot_out, preferred_element_type=jnp.float32)
-    comb_logit = combine * (comb_grad - jnp.sum(combine * comb_grad, axis=2, keepdims=True))
-    disp_grad = jnp.einsum("bpd,bsd->bps", tokens, slot_dx, preferred_element_type=jnp.float32)
-    disp_logit = dispatch * (disp_grad - jnp.sum(dispatch * disp_grad, axis=1, keepdims=True))
-    logit_grad = (comb_logit + disp_logit).astype(jnp.bfloat16)
-    grad_tokens = (
-        jnp.einsum("bps,bsd->bpd", dispatch_low, slot_dx, preferred_element_type=jnp.float32)
-        + jnp.einsum("bps,ds->bpd", logit_grad, slot_keys, preferred_element_type=jnp.float32)
-    ).astype(jnp.bfloat16)
-    key_terms = jnp.einsum("bpd,bps->sd", tokens, logit_grad, preferred_element_type=jnp.float32)
-    tiles = key_terms.reshape(slots // 8, 8, width // 128, 128).transpose(0, 2, 1, 3)
-    summed = sum_over_devices(tiles.reshape(-1, 8, 128))
-    summed = summed.reshape(slots // 8, width // 128, 8, 128).transpose(0, 2, 1, 3)
-    grad_keys = summed.reshape(slots, width).T
-    return (grad_tokens, grad_keys, grad_w_in, grad_w_out)
+    grad_tokens, grad_keys = combine_gradients(tokens, grad_out, slot_keys.T, back)
+    return (grad_tokens, grad_keys.T, grad_w_in, grad_w_out)
 
 
 def solution(mesh):

time: 175 us -> 160 us (0.914)
  matrix products: 9.6 us -> 2.56 us
  Pallas kernels: 154 us -> 148 us
    dot_general x5 -> x0, matrix products: 7.56 us -> none  [the longest x1 3.56 us: local(): jnp.einsum('bps,bsd->bpd', dispatch_low, slot_dx, preferred_element_type=...]
    pallas_call x1, Pallas kernels: 26.2 us -> 20.1 us  [combine_gradients(): pl.pallas_call(combine_kernel, out_shape=(jax.ShapeDtypeStruct(tokens.sha...]
    unnamed x12 -> x16, local copies, waits for them, and re-layouts: 4.5 us -> 6.58 us
where the time goes in v4:
time: 160 us
  Pallas kernels  148 us (92%)
  local copies, waits for them, and re-layouts  7.89 us (5%)
  matrix products  2.56 us (2%)
    pallas_call x1, Pallas kernels, expert_exchange(): pl.pallas_call(exchange_kernel, out_shape=(jax.ShapeDtypeStruct(pieces.sh...  128 us
    pallas_call x1, Pallas kernels, combine_gradients(): pl.pallas_call(combine_kernel, out_shape=(jax.ShapeDtypeStruct(tokens.sha...  20.1 us
    unnamed x16, local copies, waits for them, and re-layouts  6.58 us

profile of v4, /device:TPU:1, one launch (start us, length us, event | category | flops | bytes accessed | tf_op | source)
XLA Modules:
  0.0 159.7 jit_solution(16451624736672498522)
XLA Ops:
  0.6 0.0 copy-start.1
  0.6 1.9 %fusion.6 = f32[2,256,32]{1,2,0:T(8,128)S(1)} fusion(bf16[2,256,1280]{2,1,0:T(8,128)(2,1)} %tokens_ref.1, bf16[1280,32]{0,1:T(8,128)(2,1)} %param.6), kind=kOutput, calls=%fused_computation.9 | convolution fusion | flops 41943040 | bytes 1458176 | tf_op jit(solution)/shard_map/bpd,ds->bps/dot_general | solution.py:491
  2.5 0.0 copy-start
  2.5 0.2 fusion.13
  2.8 0.0 copy-done.1
  2.8 0.3 convolution_convert_fusion
  3.1 0.1 stack.10
  3.2 0.2 copy.10
  3.3 0.5 copy-done
  3.9 0.4 convolution_convert_fusion.1
  4.2 0.1 stack.9
  4.3 0.2 copy.9
  4.5 0.4 maximum_bitcast_fusion
  4.9 0.8 reshape.20.pieces_ref
  5.8 0.0 copy-start.2
  5.8 127.8 %experts.1 = (bf16[8,2,16,640]{3,2,1,0:T(8,128)(2,1)}, bf16[2,320,1280]{2,1,0:T(8,128)(2,1)}, bf16[2,320,1280]{2,1,0:T(8,128)(2,1)}) custom-call(bf16[8,2,16,640]{3,2,1,0:T(8,128)(2,1)} %reshape.20.pieces_ref, bf16[2,320,1280]{2,1,0:T(8,128)(2,1)} %bitcast.18, bf16[2,320,1280]{2,1,0:T(8,128)(2,1)} %w_out_ref.1), custom_call_target="tpu_custom_call" | custom-call | tf_op jit(solution)/shard_map/experts/pallas_call | solution.py:458
  133.6 0.0 copy-done.2
  133.6 0.0 copy-start.3
  133.6 1.0 copy-done.3
  134.5 20.1 %combine.1 = (bf16[2,256,1280]{2,1,0:T(8,128)(2,1)S(1)}, f32[32,1280]{1,0:T(8,128)S(1)}) custom-call(bf16[2,256,1280]{2,1,0:T(8,128)(2,1)S(1)} %copy-done, bf16[2,256,1280]{2,1,0:T(8,128)(2,1)S(1)} %copy-done.1, bf16[32,1280]{1,0:T(8,128)(2,1)S(1)} %bitcast.16, bf16[8,2,16,640]{3,2,1,0:T(8,128)(2,1)S(1)} %copy-done.3), custom_call_target="tpu_custom_call" | custom-call | tf_op jit(solution)/shard_map/combine/pallas_call | solution.py:197
  154.6 0.0 copy-start.5
  154.6 1.1 copy.15
  155.7 0.7 copy.16
  156.3 0.2 copy-done.5
  156.5 0.0 copy-start.4
  156.5 1.2 copy.17
  157.7 0.9 copy-done.4
  158.5 1.2 copy.18
  (1 shorter events, 0.0 us)
Async XLA Ops:
  0.6 2.1 %copy-start.1 = (bf16[2,256,1280]{2,1,0:T(8,128)(2,1)S(1)}, bf16[2,256,1280]{2,1,0:T(8,128)(2,1)}, u32[]{:S(2)}) copy-start(bf16[2,256,1280]{2,1,0:T(8,128)(2,1)} %grad_ref.1) | copy-start | bytes 3932164
  2.5 1.3 copy-start
  5.8 127.8 %copy-start.2 = (bf16[1280,32]{0,1:T(8,128)(2,1)S(1)}, bf16[1280,32]{0,1:T(8,128)(2,1)}, u32[]{:S(2)}) copy-start(bf16[1280,32]{0,1:T(8,128)(2,1)} %param.6) | copy-start | bytes 245764
  133.6 1.0 copy-start.3
  154.6 1.9 %copy-start.5 = (bf16[2,320,1280]{2,1,0:T(8,128)(2,1)S(1)}, bf16[2,320,1280]{2,1,0:T(8,128)(2,1)}, u32[]{:S(2)}) copy-start(bf16[2,320,1280]{2,1,0:T(8,128)(2,1)} %get-tuple-element.12) | copy-start | bytes 4915204
  156.5 2.0 %copy-start.4 = (bf16[2,320,1280]{2,1,0:T(8,128)(2,1)S(1)}, bf16[2,320,1280]{2,1,0:T(8,128)(2,1)}, u32[]{:S(2)}) copy-start(bf16[2,320,1280]{2,1,0:T(8,128)(2,1)} %get-tuple-element.21) | copy-start | bytes 4915204

commit v5 on v4

--- a/solution.py
+++ b/solution.py
@@ -225,11 +225,11 @@
 
 
 def exchange_kernel(
-    pieces_ref, w_in_ref, w_out_ref,
+    tokens_ref, grad_ref, keys_ref, w_in_hbm, w_out_hbm,
     back_ref, grad_in_ref, grad_out_ref,
-    landed, own, rows, part, hid, pre, from_left, from_right, sum_left, sum_right, sum_z, ready,
+    w_in_ref, w_out_ref, pieces_ref, landed, own, rows, part, hid, pre, from_left, from_right, sum_left, sum_right, sum_z, ready,
     send_x, recv_x, send_b, recv_b, send_z, recv_z, send_s, recv_s,
-    send_y, recv_y, send_h, recv_h, send_f, recv_f, send_p, recv_p,
+    send_y, recv_y, send_h, recv_h, send_f, recv_f, send_p, recv_p, fetched,
 ):
     row, col = lax.axis_index("dp"), lax.axis_index("expert")
     yy = lax.rem(row, Y)
@@ -262,6 +262,35 @@
         )
     pl.semaphore_signal(barrier, inc=1, device_id=right, device_id_type=MESH)
     pl.semaphore_signal(barrier, inc=1, device_id=left, device_id_type=MESH)
+    w_in_copy = pltpu.make_async_copy(w_in_hbm, w_in_ref, fetched.at[0])
+    w_out_copy = pltpu.make_async_copy(w_out_hbm, w_out_ref, fetched.at[1])
+    w_in_copy.start()
+    w_out_copy.start()
+
+    size = GROUP * PIECE
+    r = lax.broadcasted_iota(jnp.int32, (size, size), 0)
+    c = lax.broadcasted_iota(jnp.int32, (size, size), 1)
+    home = ((r >> 3) & 1) * 128 + ((r >> 2) & 1) * 64 + (r & 1) * 32
+    home = home + (r >> 6) * 8 + ((r >> 4) & 1) * 4 + ((r >> 5) & 1) * 2 + ((r >> 1) & 1)
+    order = (c == home).astype(jnp.bfloat16)
+    slots = [[None, None], [None, None]]
+    for i in range(2):
+        logits = times(keys_ref[...], tokens_ref[i], ((1,), (1,)))
+        dispatch, combine = soft(logits, 1), soft(logits, 0)
+        for t, (share, x) in enumerate(((dispatch, tokens_ref), (combine, grad_ref))):
+            seen = times(share.astype(jnp.bfloat16), x[i], ((1,), (0,)))
+            slots[t][i] = seen.astype(jnp.bfloat16)
+    stack = jnp.concatenate(
+        [
+            slots[t][i][:, h * HALF : (h + 1) * HALF]
+            for h in range(2)
+            for t in range(2)
+            for i in range(2)
+        ],
+        axis=0,
+    )
+    pieces = times(order, stack, ((1,), (0,))).astype(jnp.bfloat16)
+    pieces_ref[...] = pieces.reshape(SIDE, 2, PIECE, HALF)
     pl.semaphore_wait(barrier, 2 * (SIDE - 1) + 2)
 
     def piece_out(o):
@@ -384,6 +413,8 @@
     fetch(0)
     fetch(1)
     spread(0)
+    w_in_copy.wait()
+    w_out_copy.wait()
     for q in range(last + 1):
         fetch(q + 2)
         spread(q + 1)
@@ -449,7 +480,8 @@
             near(q, d).wait_send()
 
 
-def expert_exchange(pieces, w_in_turned, w_out):
+def expert_exchange(tokens, grad_out, keys_turned, w_in_turned, w_out):
+    pieces = (SIDE, 2, PIECE, HALF)
     block = (2, 2, SEEN, D)
     slabs = 2 * Z
     bf16 = jnp.bfloat16
@@ -458,14 +490,17 @@
     return pl.pallas_call(
         exchange_kernel,
         out_shape=(
-            jax.ShapeDtypeStruct(pieces.shape, bf16),
+            jax.ShapeDtypeStruct(pieces, bf16),
             jax.ShapeDtypeStruct(w_out.shape, bf16),
             jax.ShapeDtypeStruct(w_out.shape, bf16),
         ),
-        in_specs=[vmem] * 3,
+        in_specs=[vmem] * 3 + [pl.BlockSpec(memory_space=pl.ANY)] * 2,
         out_specs=(vmem,) * 3,
         scratch_shapes=[
-            pltpu.VMEM(pieces.shape, bf16),
+            pltpu.VMEM(w_out.shape, bf16),
+            pltpu.VMEM(w_out.shape, bf16),
+            pltpu.VMEM(pieces, bf16),
+            pltpu.VMEM(pieces, bf16),
             pltpu.VMEM((2,) + block, bf16),
             pltpu.VMEM((slabs, Y) + block, bf16),
             pltpu.VMEM((slabs, Y) + block, bf16),
@@ -476,36 +511,25 @@
             pltpu.VMEM((slabs,) + block, bf16),
             pltpu.VMEM((slabs,) + block, bf16),
             pltpu.VMEM((slabs,) + block, bf16),
-            pltpu.VMEM(pieces.shape, bf16),
+            pltpu.VMEM(pieces, bf16),
         ]
         + [dma((SIDE,))] * 8
-        + [dma((slabs, 2))] * 8,
+        + [dma((slabs, 2))] * 8
+        + [dma((2,))],
         compiler_params=pltpu.CompilerParams(
             collective_id=0, has_side_effects=True, vmem_limit_bytes=56 * 1024 * 1024
         ),
         name="experts",
-    )(pieces, w_in_turned, w_out)
+    )(tokens, grad_out, keys_turned, w_in_turned, w_out)
 
 
 def local(tokens, slot_keys, w_in, w_out, grad_out):
-    logits = jnp.einsum("bpd,ds->bps", tokens, slot_keys, preferred_element_type=jnp.float32)
-    dispatch = jax.nn.softmax(logits, axis=1)
-    combine = jax.nn.softmax(logits, axis=2)
-    dispatch_low = dispatch.astype(jnp.bfloat16)
-    combine_low = combine.astype(jnp.bfloat16)
-    slot_in = jnp.einsum(
-        "bps,bpd->bsd", dispatch_low, tokens, preferred_element_type=jnp.float32
-    ).astype(jnp.bfloat16)
-    slot_grad = jnp.einsum(
-        "bps,bpd->bsd", combine_low, grad_out, preferred_element_type=jnp.float32
-    ).astype(jnp.bfloat16)
-    images, slots, width = slot_in.shape
-    pieces = jnp.stack([slot_in, slot_grad]).reshape(2, images, 4, 2, 2, slots // GROUP, 2, HALF)
-    pieces = pieces.transpose(2, 4, 3, 6, 0, 5, 1, 7).reshape(SIDE, 2, PIECE, HALF)
-    back, grad_w_in, grad_w_out = expert_exchange(pieces, w_in.transpose(0, 2, 1), w_out)
-    grad_w_in = grad_w_in.transpose(0, 2, 1)
-    grad_tokens, grad_keys = combine_gradients(tokens, grad_out, slot_keys.T, back)
-    return (grad_tokens, grad_keys.T, grad_w_in, grad_w_out)
+    keys_turned = slot_keys.T
+    back, grad_w_in, grad_w_out = expert_exchange(
+        tokens, grad_out, keys_turned, w_in.transpose(0, 2, 1), w_out
+    )
+    grad_tokens, grad_keys = combine_gradients(tokens, grad_out, keys_turned, back)
+    return (grad_tokens, grad_keys.T, grad_w_in.transpose(0, 2, 1), grad_w_out)
 
 
 def solution(mesh):

time: 160 us -> 155 us (0.969)
  matrix products: 2.56 us -> 0 us
  local copies, waits for them, and re-layouts: 7.89 us -> 6.06 us
    dot_general x3 -> x0, matrix products: 2.56 us -> none  [the longest x1 1.89 us: local(): jnp.einsum('bpd,ds->bps', tokens, slot_keys, preferred_element_type=jnp.f...]
where the time goes in v5:
time: 155 us
  Pallas kernels  148 us (95%)
  local copies, waits for them, and re-layouts  6.06 us (4%)
    pallas_call x1, Pallas kernels, expert_exchange(): pl.pallas_call(exchange_kernel, out_shape=(jax.ShapeDtypeStruct(pieces, b...  128 us
    pallas_call x1, Pallas kernels, combine_gradients(): pl.pallas_call(combine_kernel, out_shape=(jax.ShapeDtypeStruct(tokens.sha...  20.2 us
    unnamed x16, local copies, waits for them, and re-layouts  6.06 us

profile of v5, /device:TPU:1, one launch (start us, length us, event | category | flops | bytes accessed | tf_op | source)
XLA Modules:
  0.0 154.8 jit_solution(8403891622250473398)
XLA Ops:
  0.6 0.0 copy-start
  0.6 0.0 copy-start.1
  0.7 0.0 copy-start.3
  0.7 127.8 %experts.1 = (bf16[8,2,16,640]{3,2,1,0:T(8,128)(2,1)}, bf16[2,320,1280]{2,1,0:T(8,128)(2,1)}, bf16[2,320,1280]{2,1,0:T(8,128)(2,1)}) custom-call(bf16[2,256,1280]{2,1,0:T(8,128)(2,1)} %tokens_ref.3, bf16[2,256,1280]{2,1,0:T(8,128)(2,1)} %grad_ref.3, bf16[32,1280]{1,0:T(8,128)(2,1)} %bitcast.4, bf16[2,320,1280]{2,1,0:T(8,128)(2,1)} %bitcast.7, ...), custom_call_target="tpu_custom_call" | custom-call | tf_op jit(solution)/shard_map/experts/pallas_call | solution.py:490
  128.4 0.0 copy-done
  128.4 0.0 copy-done.1
  128.5 0.0 copy-done.3
  128.5 0.0 copy-start.2
  128.5 1.0 copy-done.2
  129.4 20.2 %combine.1 = (bf16[2,256,1280]{2,1,0:T(8,128)(2,1)S(1)}, f32[32,1280]{1,0:T(8,128)S(1)}) custom-call(bf16[2,256,1280]{2,1,0:T(8,128)(2,1)S(1)} %copy-done, bf16[2,256,1280]{2,1,0:T(8,128)(2,1)S(1)} %copy-done.1, bf16[32,1280]{1,0:T(8,128)(2,1)S(1)} %bitcast.5, bf16[8,2,16,640]{3,2,1,0:T(8,128)(2,1)S(1)} %copy-done.2), custom_call_target="tpu_custom_call" | custom-call | tf_op jit(solution)/shard_map/combine/pallas_call | solution.py:197
  149.7 0.0 copy-start.5
  149.7 1.1 copy.13
  150.8 0.7 copy.14
  151.4 0.2 copy-done.5
  151.6 0.0 copy-start.4
  151.6 1.2 copy.15
  152.8 0.9 copy-done.4
  153.6 1.2 copy.16
Async XLA Ops:
  0.6 127.8 %copy-start = (bf16[2,256,1280]{2,1,0:T(8,128)(2,1)S(1)}, bf16[2,256,1280]{2,1,0:T(8,128)(2,1)}, u32[]{:S(2)}) copy-start(bf16[2,256,1280]{2,1,0:T(8,128)(2,1)} %tokens_ref.3) | copy-start | bytes 3932164
  0.6 127.8 %copy-start.1 = (bf16[2,256,1280]{2,1,0:T(8,128)(2,1)S(1)}, bf16[2,256,1280]{2,1,0:T(8,128)(2,1)}, u32[]{:S(2)}) copy-start(bf16[2,256,1280]{2,1,0:T(8,128)(2,1)} %grad_ref.3) | copy-start | bytes 3932164
  0.7 127.8 %copy-start.3 = (bf16[1280,32]{0,1:T(8,128)(2,1)S(1)}, bf16[1280,32]{0,1:T(8,128)(2,1)}, u32[]{:S(2)}) copy-start(bf16[1280,32]{0,1:T(8,128)(2,1)} %param.6) | copy-start | bytes 245764
  128.5 1.0 copy-start.2
  149.7 1.9 %copy-start.5 = (bf16[2,320,1280]{2,1,0:T(8,128)(2,1)S(1)}, bf16[2,320,1280]{2,1,0:T(8,128)(2,1)}, u32[]{:S(2)}) copy-start(bf16[2,320,1280]{2,1,0:T(8,128)(2,1)} %get-tuple-element.12) | copy-start | bytes 4915204
  151.6 2.0 %copy-start.4 = (bf16[2,320,1280]{2,1,0:T(8,128)(2,1)S(1)}, bf16[2,320,1280]{2,1,0:T(8,128)(2,1)}, u32[]{:S(2)}) copy-start(bf16[2,320,1280]{2,1,0:T(8,128)(2,1)} %get-tuple-element.21) | copy-start | bytes 4915204

commit v6 on v5

--- a/solution.py
+++ b/solution.py
@@ -15,7 +15,7 @@
 TILES = D // 128
 SIDE = 8
 SEEN = 16
-AWAY = (0, 1, 7, 2, 6, 3, 5, 4)
+AWAY = (0, 1, 2, 6, 4, 3, 5, 7)
 PIECE = 16
 
 INV_ROOT2 = 0.7071067811865476
@@ -226,8 +226,8 @@
 
 def exchange_kernel(
     tokens_ref, grad_ref, keys_ref, w_in_hbm, w_out_hbm,
-    back_ref, grad_in_ref, grad_out_ref,
-    w_in_ref, w_out_ref, pieces_ref, landed, own, rows, part, hid, pre, from_left, from_right, sum_left, sum_right, sum_z, ready,
+    back_ref, grad_in_hbm, grad_out_hbm,
+    w_in_ref, w_out_ref, grad_in_ref, grad_out_ref, pieces_ref, landed, own, rows, part, hid, pre, from_left, from_right, sum_left, sum_right, sum_z, ready,
     send_x, recv_x, send_b, recv_b, send_z, recv_z, send_s, recv_s,
     send_y, recv_y, send_h, recv_h, send_f, recv_f, send_p, recv_p, fetched,
 ):
@@ -391,15 +391,13 @@
             along_z_back(q).start()
 
     last = len(AWAY) - 1
-    for q in range(1, 4):
+    for q in range(1, last + 1):
         along_z(q).start()
     rows[zz, yy] = own[zz // Z]
 
     def fetch(q):
         if 1 <= q <= last:
             along_z(q).wait_recv()
-            if q + 3 <= last:
-                along_z(q + 3).start()
         if q <= last:
             for d in range(2):
                 along_y(q, d).start()
@@ -427,9 +425,14 @@
             pass_on(q - 1)
         if q >= 3:
             collect(q - 2)
-    begin(0)
-
-    for s in range(2):
+
+    def weight_copies(s):
+        return [
+            pltpu.make_async_copy(ours.at[s], out.at[s], fetched.at[2 + 2 * s + k])
+            for k, (ours, out) in enumerate(((grad_in_ref, grad_in_hbm), (grad_out_ref, grad_out_hbm)))
+        ]
+
+    def weight_grads(s):
         p_all = pre[s].reshape(2 * Z * Y * SEEN, HID)
         h_all = hid[s].reshape(2 * Z * Y * SEEN, HID)
         for k in range(0, D, 256):
@@ -437,10 +440,15 @@
             g = rows[:, :, 1, s, :, k : k + 256].reshape(2 * Z * Y * SEEN, 256)
             grad_in_ref[s, :, k : k + 256] = times(p_all, x, ((0,), (0,))).astype(jnp.bfloat16)
             grad_out_ref[s, :, k : k + 256] = times(h_all, g, ((0,), (0,))).astype(jnp.bfloat16)
-        if s == 0:
-            pass_on(last)
-            collect(last - 1)
-            pass_on(0)
+        for copy in weight_copies(s):
+            copy.start()
+
+    weight_grads(0)
+    pass_on(last)
+    begin(0)
+    collect(last - 1)
+    weight_grads(1)
+    pass_on(0)
     collect(last)
     collect(0)
 
@@ -466,6 +474,9 @@
     for o in range(1, SIDE):
         piece_back(o).wait_recv()
 
+    for s in range(2):
+        for copy in weight_copies(s):
+            copy.wait()
     for o in range(1, SIDE):
         piece_out(o).wait_send()
         piece_back(o).wait_send()
@@ -495,8 +506,10 @@
             jax.ShapeDtypeStruct(w_out.shape, bf16),
         ),
         in_specs=[vmem] * 3 + [pl.BlockSpec(memory_space=pl.ANY)] * 2,
-        out_specs=(vmem,) * 3,
+        out_specs=(vmem,) + (pl.BlockSpec(memory_space=pl.ANY),) * 2,
         scratch_shapes=[
+            pltpu.VMEM(w_out.shape, bf16),
+            pltpu.VMEM(w_out.shape, bf16),
             pltpu.VMEM(w_out.shape, bf16),
             pltpu.VMEM(w_out.shape, bf16),
             pltpu.VMEM(pieces, bf16),
@@ -515,12 +528,39 @@
         ]
         + [dma((SIDE,))] * 8
         + [dma((slabs, 2))] * 8
-        + [dma((2,))],
+        + [dma((6,))],
         compiler_params=pltpu.CompilerParams(
             collective_id=0, has_side_effects=True, vmem_limit_bytes=56 * 1024 * 1024
         ),
         name="experts",
     )(tokens, grad_out, keys_turned, w_in_turned, w_out)
+
+
+def settle_kernel(*refs):
+    count = (len(refs) - 1) // 2
+    done = refs[-1]
+    copies = [
+        pltpu.make_async_copy(src.at[k], dst.at[k], done.at[j, k])
+        for j, (src, dst) in enumerate(zip(refs[:count], refs[count : 2 * count]))
+        for k in range(2)
+    ]
+    for copy in copies:
+        copy.start()
+    for copy in copies:
+        copy.wait()
+
+
+def settled(*arrays):
+    anywhere = pl.BlockSpec(memory_space=pl.ANY)
+    return pl.pallas_call(
+        settle_kernel,
+        out_shape=tuple(jax.ShapeDtypeStruct(a.shape, a.dtype) for a in arrays),
+        in_specs=[pl.BlockSpec(memory_space=pltpu.VMEM)] * len(arrays),
+        out_specs=(anywhere,) * len(arrays),
+        scratch_shapes=[pltpu.SemaphoreType.DMA((len(arrays), 2))],
+        compiler_params=pltpu.CompilerParams(vmem_limit_bytes=16 * 1024 * 1024),
+        name="settle",
+    )(*arrays)
 
 
 def local(tokens, slot_keys, w_in, w_out, grad_out):
@@ -529,6 +569,10 @@
         tokens, grad_out, keys_turned, w_in.transpose(0, 2, 1), w_out
     )
     grad_tokens, grad_keys = combine_gradients(tokens, grad_out, keys_turned, back)
+    grad_tokens, grad_keys, grad_w_in, grad_w_out = settled(
+        grad_tokens, grad_keys.reshape(2, SLOTS // 2, D), grad_w_in, grad_w_out
+    )
+    grad_keys = grad_keys.reshape(SLOTS, D)
     return (grad_tokens, grad_keys.T, grad_w_in.transpose(0, 2, 1), grad_w_out)
 
 

time: 155 us -> 150 us (0.968)
  local copies, waits for them, and re-layouts: 6.06 us -> 2.52 us
  Pallas kernels: 148 us -> 146 us
    pallas_call x1, Pallas kernels: 128 us -> 124 us  [expert_exchange(): pl.pallas_call(exchange_kernel, out_shape=(jax.ShapeDtypeStruct(pieces, b...]
    unnamed x16 -> x12, local copies, waits for them, and re-layouts: 6.06 us -> 2.52 us
    pallas_call x0 -> x1, Pallas kernels: none -> 2.25 us  [settled(): pl.pallas_call(settle_kernel, out_shape=tuple((jax.ShapeDtypeStruct(a.sha...]
where the time goes in v6:
time: 150 us
  Pallas kernels  146 us (97%)
  local copies, waits for them, and re-layouts  2.52 us (2%)
    pallas_call x1, Pallas kernels, expert_exchange(): pl.pallas_call(exchange_kernel, out_shape=(jax.ShapeDtypeStruct(pieces, b...  124 us
    pallas_call x1, Pallas kernels, combine_gradients(): pl.pallas_call(combine_kernel, out_shape=(jax.ShapeDtypeStruct(tokens.sha...  20 us

profile of v6, /device:TPU:1, one launch (start us, length us, event | category | flops | bytes accessed | tf_op | source)
XLA Modules:
  0.0 149.6 jit_solution(17399187279487121970)
XLA Ops:
  0.6 0.0 copy-start
  0.6 0.0 copy-start.1
  0.7 0.0 copy-start.5
  0.7 123.9 %experts.1 = (bf16[8,2,16,640]{3,2,1,0:T(8,128)(2,1)}, bf16[2,320,1280]{2,1,0:T(8,128)(2,1)}, bf16[2,320,1280]{2,1,0:T(8,128)(2,1)}) custom-call(bf16[2,256,1280]{2,1,0:T(8,128)(2,1)} %tokens_ref.3, bf16[2,256,1280]{2,1,0:T(8,128)(2,1)} %grad_ref.3, bf16[32,1280]{1,0:T(8,128)(2,1)} %bitcast.7, bf16[2,320,1280]{2,1,0:T(8,128)(2,1)} %bitcast.10, ...), custom_call_target="tpu_custom_call" | custom-call | tf_op jit(solution)/shard_map/experts/pallas_call | solution.py:501
  124.6 0.0 copy-start.2
  124.6 0.0 copy-done
  124.6 0.0 copy-done.1
  124.6 0.0 copy-done.5
  124.6 0.0 copy-start.4
  124.6 1.1 copy-done.4
  125.7 20.0 %combine.1 = (bf16[2,256,1280]{2,1,0:T(8,128)(2,1)S(1)}, f32[32,1280]{1,0:T(8,128)S(1)}) custom-call(bf16[2,256,1280]{2,1,0:T(8,128)(2,1)S(1)} %copy-done, bf16[2,256,1280]{2,1,0:T(8,128)(2,1)S(1)} %copy-done.1, bf16[32,1280]{1,0:T(8,128)(2,1)S(1)} %bitcast.8, bf16[8,2,16,640]{3,2,1,0:T(8,128)(2,1)S(1)} %copy-done.4), custom_call_target="tpu_custom_call" | custom-call | tf_op jit(solution)/shard_map/combine/pallas_call | solution.py:197
  145.8 0.0 copy-done.2
  145.8 0.0 copy-start.3
  145.8 1.4 copy-done.3
  147.2 2.3 %settle.1 = (bf16[2,256,1280]{2,1,0:T(8,128)(2,1)}, f32[2,16,1280]{2,1,0:T(8,128)}, bf16[2,320,1280]{2,1,0:T(8,128)(2,1)}, bf16[2,320,1280]{2,1,0:T(8,128)(2,1)}) custom-call(bf16[2,256,1280]{2,1,0:T(8,128)(2,1)S(1)} %get-tuple-element.14.refs_0_, f32[2,16,1280]{2,1,0:T(8,128)S(1)} %bitcast.9, bf16[2,320,1280]{2,1,0:T(8,128)(2,1)S(1)} %copy-done.2, ...), custom_call_target="tpu_custom_call" | custom-call | tf_op jit(solution)/shard_map/settle/pallas_call | solution.py:555
Async XLA Ops:
  0.6 124.0 %copy-start = (bf16[2,256,1280]{2,1,0:T(8,128)(2,1)S(1)}, bf16[2,256,1280]{2,1,0:T(8,128)(2,1)}, u32[]{:S(2)}) copy-start(bf16[2,256,1280]{2,1,0:T(8,128)(2,1)} %tokens_ref.3) | copy-start | bytes 3932164
  0.6 124.0 %copy-start.1 = (bf16[2,256,1280]{2,1,0:T(8,128)(2,1)S(1)}, bf16[2,256,1280]{2,1,0:T(8,128)(2,1)}, u32[]{:S(2)}) copy-start(bf16[2,256,1280]{2,1,0:T(8,128)(2,1)} %grad_ref.3) | copy-start | bytes 3932164
  0.7 124.0 %copy-start.5 = (bf16[1280,32]{0,1:T(8,128)(2,1)S(1)}, bf16[1280,32]{0,1:T(8,128)(2,1)}, u32[]{:S(2)}) copy-start(bf16[1280,32]{0,1:T(8,128)(2,1)} %param.6) | copy-start | bytes 245764
  124.6 21.2 %copy-start.2 = (bf16[2,320,1280]{2,1,0:T(8,128)(2,1)S(1)}, bf16[2,320,1280]{2,1,0:T(8,128)(2,1)}, u32[]{:S(2)}) copy-start(bf16[2,320,1280]{2,1,0:T(8,128)(2,1)} %get-tuple-element.16.refs_2_) | copy-start | bytes 4915204
  124.6 1.1 copy-start.4
  145.8 1.4 copy-start.3
